TPU v7x, 128 devices: a whole 4x4x4 slice. The times are simulated.
128 devices in a mesh: dp: 16 (over y, z), ctx: 8 (over x, core).
Axes of the slice: x: 4, y: 4, z: 4, core: 2. Of those that a mesh axis runs over, the one named last changes fastest.
Arguments:
- queries: bfloat16 [16, 1024, 1024], P('dp', 'ctx'), may hold values from -48 to 48
- keys: bfloat16 [16, 1024, 1024], P('dp', 'ctx'), may hold values from -8 to 8
- values: bfloat16 [16, 1024, 1024], P('dp', 'ctx'), may hold values from -6 to 6
- directions: bfloat16 [16, 1024, 1024], P('dp', 'ctx'), may hold values from -6 to 6
- beta_logits: float32 [16, 8, 1024], P('dp', None, 'ctx'), may hold values from -24 to 10
- out_proj: bfloat16 [1024, 4096], replicated, may hold values from -0.1875 to 0.1875
- out_grad: bfloat16 [16, 1024, 4096], P('dp', 'ctx'), may hold values from -6 to 6
- doc_lengths: int32 [16, 4], P('dp'), may hold values from 1 to 640, 1024 in all within a row
Outputs:
- grad_queries: bfloat16 [16, 1024, 1024], P('dp', 'ctx')
- grad_keys: bfloat16 [16, 1024, 1024], P('dp', 'ctx')
- grad_values: bfloat16 [16, 1024, 1024], P('dp', 'ctx')
- grad_directions: bfloat16 [16, 1024, 1024], P('dp', 'ctx')
- grad_beta: float32 [16, 8, 1024], P('dp', None, 'ctx')
- grad_proj: float32 [1024, 4096], P(('dp', 'ctx'))
All inputs are finite; a program needn't handle non-finite values.
Results may differ from a plain program's by a relative error of at most 0.015.
Values may be sent and summed in bfloat16 or wider, within the bound.
A program may use at most 128 MiB of HBM per device.

v0:
```python
import functools

import jax
import jax.numpy as jnp
from jax import lax
from jax.sharding import PartitionSpec as P

highest = lax.Precision.HIGHEST


def passed_along(value, axis, steps):
    count = lax.axis_size(axis)
    leading, last = (max(0, -steps), min(count, count - steps))
    return lax.ppermute(value, axis, [(source, source + steps) for source in range(leading, last)])


def block_parts(query, key_rows, direction, beta):
    size = query.shape[0]
    order = jnp.arange(size, dtype=jnp.int32)
    within = order[None, :] <= order[:, None]
    before = order[:, None] > order[None, :]
    gram = jnp.dot(direction, direction.T, precision=highest)
    unit = jnp.eye(size, dtype=query.dtype) + jnp.where(before, beta[:, None] * gram, 0.0)
    solved = jax.scipy.linalg.solve_triangular(
        unit, beta[:, None] * direction, lower=True, unit_diagonal=True
    )
    across = jnp.where(within, jnp.dot(query, direction.T, precision=highest), 0.0)
    query_bar = query - jnp.dot(across, solved, precision=highest)
    right = jnp.where(
        before, beta[:, None] * jnp.dot(direction, key_rows.T, precision=highest), 0.0
    )
    coeffs = jax.scipy.linalg.solve_triangular(unit, right, lower=True, unit_diagonal=True)
    key_tilde = key_rows - jnp.dot(coeffs.T, direction, precision=highest)
    inner = jnp.dot(query, key_rows.T, precision=highest) - jnp.dot(
        across, coeffs, precision=highest
    )
    transform = jnp.eye(direction.shape[1], dtype=query.dtype) - jnp.dot(
        direction.T, solved, precision=highest
    )
    return (query_bar, key_tilde, transform, inner)


def block_local(query, keys_in, raw_dirs, logits):
    size = query.shape[0]
    heads = logits.shape[0]

    def split(matrix):
        return matrix.reshape(size, heads, -1).transpose(1, 0, 2)

    direction = split(raw_dirs)
    direction = direction * lax.rsqrt(
        jnp.sum(direction * direction, axis=-1, keepdims=True) + 1e-06
    )
    beta = 2.0 * jax.nn.sigmoid(logits)
    return jax.vmap(block_parts)(split(query), split(keys_in), direction, beta)


def doc_ids(lengths, start, size):
    ends = jnp.cumsum(lengths)
    places = start + jnp.arange(size, dtype=jnp.int32)
    return jnp.sum((ends[None, :] <= places[:, None]).astype(jnp.int32), axis=1)


def per_device(queries, keys, values, directions, beta_logits, out_proj, out_grad, doc_lengths):
    width = lax.axis_size("ctx")
    place = lax.axis_index("ctx")
    size = queries.shape[1]
    heads = beta_logits.shape[1]
    hidden = queries.shape[2]
    hdim = hidden // heads
    scale = hdim ** (-0.5)
    lengths = doc_lengths[0]
    value_rows = values[0]
    parts, pullback = jax.vjp(
        block_local,
        queries[0].astype(jnp.float32),
        keys[0].astype(jnp.float32),
        directions[0].astype(jnp.float32),
        beta_logits[0],
    )
    query_bar, key_tilde, transform, inner = parts
    query_half = query_bar.astype(jnp.bfloat16)
    key_half = key_tilde.astype(jnp.bfloat16)
    matrix_half = transform.astype(jnp.bfloat16)
    received = [(key_half, value_rows)]
    current, value_now = (key_half, value_rows)
    for step in range(1, width):
        current, value_now = passed_along((current, value_now), "ctx", 1)
        received.append((current, value_now))
        if step + 1 < width:
            current = jnp.einsum(
                "hlk,hmk->hlm", current, matrix_half, preferred_element_type=jnp.float32
            ).astype(jnp.bfloat16)
    own_ids = doc_ids(lengths, place * size, size)
    order = jnp.arange(size, dtype=jnp.int32)
    causal = (order[None, :] <= order[:, None]) & (own_ids[:, None] == own_ids[None, :])
    scores = [jnp.where(causal, inner * scale, -1e30)]
    for step in range(1, width):
        other_ids = doc_ids(lengths, (place - step) * size, size)
        allowed = (place >= step) & (own_ids[:, None] == other_ids[None, :])
        raw = (
            jnp.einsum(
                "hik,hjk->hij", query_half, received[step][0], preferred_element_type=jnp.float32
            )
            * scale
        )
        scores.append(jnp.where(allowed, raw, -1e30))
    peak = functools.reduce(jnp.maximum, [jnp.max(block, axis=-1) for block in scores])
    mass = functools.reduce(
        jnp.add, [jnp.sum(jnp.exp(block - peak[..., None]), axis=-1) for block in scores]
    )
    log_mass = peak + jnp.log(mass)
    probs = [jnp.exp(block - log_mass[..., None]) for block in scores]
    halves = [block.astype(jnp.bfloat16) for block in probs]
    value_heads = [pair[1].reshape(size, heads, hdim) for pair in received]
    output = functools.reduce(
        jnp.add,
        [
            jnp.einsum("hij,jhk->ihk", half, stacked, preferred_element_type=jnp.float32)
            for half, stacked in zip(halves, value_heads)
        ],
    )
    dense_grad = out_grad[0]
    dout = jnp.dot(dense_grad, out_proj.T, preferred_element_type=jnp.float32).astype(jnp.bfloat16)
    grad_heads = dout.reshape(size, heads, hdim)
    dprob = [
        jnp.einsum("ihk,jhk->hij", grad_heads, stacked, preferred_element_type=jnp.float32)
        for stacked in value_heads
    ]
    center = functools.reduce(
        jnp.add, [jnp.sum(block * grad, axis=-1) for block, grad in zip(probs, dprob)]
    )
    dscore = [block * (grad - center[..., None]) for block, grad in zip(probs, dprob)]
    dvalue = [
        jnp.einsum("hij,ihk->jhk", half, grad_heads, preferred_element_type=jnp.float32)
        for half in halves
    ]
    query_wide = query_half.astype(jnp.float32)
    grad_qbar = jnp.zeros((heads, size, hdim), jnp.float32)
    dkeys = [None]
    for step in range(1, width):
        block_wide = received[step][0].astype(jnp.float32)
        grad_qbar = (
            grad_qbar
            + jnp.einsum("hij,hjk->hik", dscore[step], block_wide, precision=highest) * scale
        )
        dkeys.append(
            jnp.einsum("hij,hik->hjk", dscore[step], query_wide, precision=highest) * scale
        )
    matrix_wide = matrix_half.astype(jnp.float32)
    grad_mat = jnp.zeros((heads, hdim, hdim), jnp.float32)
    carry_keys = jnp.zeros((heads, size, hdim), jnp.float32)
    carry_values = jnp.zeros((size, heads, hdim), jnp.float32)
    back_keys, back_values = (carry_keys, carry_values)
    for step in range(width - 1, -1, -1):
        if step < width - 1:
            back_keys, back_values = (
                passed_along(carry_keys.astype(jnp.bfloat16), "ctx", -1).astype(carry_keys.dtype),
                passed_along(carry_values.astype(jnp.bfloat16), "ctx", -1).astype(
                    carry_values.dtype
                ),
            )
        if step > 0:
            block_wide = received[step][0].astype(jnp.float32)
            grad_mat = grad_mat + jnp.einsum(
                "hlm,hlk->hmk", back_keys, block_wide, precision=highest
            )
            carry_keys = dkeys[step] + jnp.einsum(
                "hlm,hmk->hlk", back_keys, matrix_wide, precision=highest
            )
            carry_values = dvalue[step] + back_values
    grad_query, grad_key, grad_dir, grad_beta = pullback(
        (grad_qbar, back_keys, grad_mat, dscore[0] * scale)
    )
    grad_value = (dvalue[0] + back_values).reshape(size, hidden)
    out_half = output.reshape(size, hidden).astype(jnp.bfloat16)
    grad_proj = lax.psum_scatter(
        lax.dot_general(
            out_half, dense_grad, (((0,), (0,)), ((), ())), preferred_element_type=jnp.float32
        ),
        ("dp", "ctx"),
        scatter_dimension=0,
        tiled=True,
    )
    return (
        grad_query.astype(jnp.bfloat16)[None],
        grad_key.astype(jnp.bfloat16)[None],
        grad_value.astype(jnp.bfloat16)[None],
        grad_dir.astype(jnp.bfloat16)[None],
        grad_beta[None],
        grad_proj,
    )


def solution(mesh):
    placed = (
        P("dp", "ctx", None),
        P("dp", "ctx", None),
        P("dp", "ctx", None),
        P("dp", "ctx", None),
        P("dp", None, "ctx"),
        P(),
        P("dp", "ctx", None),
        P("dp", None),
    )
    return jax.shard_map(
        per_device,
        mesh=mesh,
        in_specs=placed,
        out_specs=(
            P("dp", "ctx", None),
            P("dp", "ctx", None),
            P("dp", "ctx", None),
            P("dp", "ctx", None),
            P("dp", None, "ctx"),
            P(("dp", "ctx"), None),
        ),
        check_vma=False,
    )
```

profile of v0, /device:TPU:0, one launch (start us, length us, event | category | flops | bytes accessed | tf_op | source)
XLA Modules:
  0.0 862.7 jit_solution(11074462585985401325)
XLA Ops:
  19.2 78.6 %custom-call.10 = f32[8,1,128,128]{2,3,1,0:T(8,128)S(1)} custom-call(f32[8,1,128,128]{3,2,1,0:T(8,128)S(1)} %add_bitcast_fusion), custom_call_target="InvertDiagBlocksLowerTriangular" | custom-call | tf_op jit(solution)/shard_map/jvp(vmap(jit(_solve_triangular)))/triangular_solve | solution.py:32
  99.0 3.0 fusion.34
  102.0 4.2 collective-permute-start
  106.2 2.1 fusion.54
  111.9 2.1 fusion.85
  116.2 2.2 fusion.35
  130.5 3.4 collective-permute-start.8
  134.2 2.2 collective-permute-start.2
  136.4 2.1 fusion.137
  138.5 3.2 collective-permute-start.9
  145.9 3.3 collective-permute-start.10
  149.5 2.2 collective-permute-start.4
  154.3 3.6 collective-permute-start.11
  160.9 3.2 collective-permute-start.12
  164.4 3.5 collective-permute-start.6
  168.3 3.5 collective-permute-start.13
  178.6 8.0 fusion.45
  186.7 7.0 convolution_convert_fusion.1
  202.5 2.0 fusion.44
  204.5 10.0 %collective-permute-start.21 = (bf16[128,8,128]{0,2,1:T(8,128)(2,1)}, bf16[128,8,128]{0,2,1:T(8,128)(2,1)}, u32[]{:S(2)}, u32[]{:S(2)}) collective-permute-start(bf16[128,8,128]{0,2,1:T(8,128)(2,1)} %fusion.44), channel_id=1, source_target_pairs={{1,0},{2,1},{3,2},{4,3},{5,4},{6,5},{7,6},{9,8},{10,9},{11,10},{12... | collective-permute-start | bytes 786440 | tf_op jit(solution)/shard_map/ppermute | solution.py:14
  267.0 2.7 collective-permute-done.23
  275.2 3.8 collective-permute-done.24
  285.4 2.7 collective-permute-done.25
  290.6 2.6 collective-permute-done.18
  298.3 5.4 collective-permute-done.19
  311.7 2.0 fusion.155
  317.9 2.0 multiply_reduce_fusion.2
  326.2 2.3 fusion.154
  329.7 2.6 multiply_reduce_fusion
  332.3 2.9 fusion.17
  336.0 2.6 multiply_reduce_fusion.1
  340.6 514.8 %reduce-scatter.2.cloned.1.call-done = f32[8,4096]{1,0:T(8,128)} async-done(((f32[1024,4096]{1,0:T(8,128)}), f32[8,4096]{1,0:T(8,128)}) %reduce-scatter.2.cloned.1.call-update) | async-done | bytes 131088 | tf_op jit(solution)/shard_map/reduce_scatter | solution.py:177
  (304 shorter events, 150.7 us)
Async XLA Ops:
  7.2 171.5 %copy-start = (bf16[1,128,4096]{2,1,0:T(8,128)(2,1)S(1)}, bf16[1,128,4096]{2,1,0:T(8,128)(2,1)}, u32[]{:S(2)}) copy-start(bf16[1,128,4096]{2,1,0:T(8,128)(2,1)} %param.18) | copy-start | bytes 3145732
  7.2 106.8 %copy-start.62 = (s32[1,4]{1,0:T(1,128)S(1)}, s32[1,4]{1,0:T(1,128)}, u32[]{:S(2)}) copy-start(s32[1,4]{1,0:T(1,128)} %param.19) | copy-start | bytes 52
  7.2 848.2 %reduce-scatter.2.cloned.1.call-start = ((), (), s32[]{:S(2)}) async-start(), calls=%async_computation.1 | async-start | bytes 16908288 | tf_op jit(solution)/shard_map/reduce_scatter | solution.py:177
  9.1 121.4 %collective-permute-start.7 = (bf16[128,1024]{0,1:T(8,128)(2,1)}, bf16[128,1024]{0,1:T(8,128)(2,1)}, u32[]{:S(2)}, u32[]{:S(2)}) collective-permute-start(bf16[128,1024]{0,1:T(8,128)(2,1)} %bitcast.19), channel_id=1, source_target_pairs={{0,1},{1,2},{2,3},{3,4},{4,5},{5,6},{6,7},{8,9},{9,10},{10,11},{11... | collective-permute-start | bytes 786440 | tf_op jit(solution)/shard_map/ppermute | solution.py:14
  102.0 16.4 %collective-permute-start = (bf16[8,128,128]{2,1,0:T(8,128)(2,1)}, bf16[8,128,128]{2,1,0:T(8,128)(2,1)}, u32[]{:S(2)}, u32[]{:S(2)}) collective-permute-start(bf16[8,128,128]{2,1,0:T(8,128)(2,1)} %fusion.34), channel_id=1, source_target_pairs={{0,1},{1,2},{2,3},{3,4},{4,5},{5,6},{6,7},{8,9},{9,10},{10,11},{11... | collective-permute-start | bytes 786440 | tf_op jit(solution)/shard_map/ppermute | solution.py:14
  120.4 13.5 %collective-permute-start.1 = (bf16[8,128,128]{2,1,0:T(8,128)(2,1)}, bf16[8,128,128]{2,1,0:T(8,128)(2,1)S(1)}, u32[]{:S(2)}, u32[]{:S(2)}) collective-permute-start(bf16[8,128,128]{2,1,0:T(8,128)(2,1)} %convolution_convert_fusion.7), channel_id=1, source_target_pairs={{0,1},{1,2},{2,3},{3,4},{4,5},{5,6},{6,7},{8,9},{9,10},{10,11},{11... | collective-permute-start | bytes 786440 | tf_op jit(solution)/shard_map/ppermute | solution.py:14
  130.5 8.0 collective-permute-start.8
  134.2 7.5 collective-permute-start.2
  138.5 7.3 collective-permute-start.9
  142.1 7.1 collective-permute-start.3
  145.9 8.4 collective-permute-start.10
  149.5 8.4 collective-permute-start.4
  154.3 6.6 collective-permute-start.11
  158.3 5.8 collective-permute-start.5
  160.9 7.3 collective-permute-start.12
  164.4 7.7 collective-permute-start.6
  168.3 9.6 %collective-permute-start.13 = (bf16[128,1024]{0,1:T(8,128)(2,1)S(1)}, bf16[128,1024]{0,1:T(8,128)(2,1)S(1)}, u32[]{:S(2)}, u32[]{:S(2)}) collective-permute-start(bf16[128,1024]{0,1:T(8,128)(2,1)S(1)} %collective-permute-done.12), channel_id=1, source_target_pairs={{0,1},{1,2},{2,3},{3,4},{4,5},{5,6},{6,7},{8,9},{9,10},{10,11},{11... | collective-permute-start | bytes 786440 | tf_op jit(solution)/shard_map/ppermute | solution.py:14
  204.5 47.8 %collective-permute-start.21 = (bf16[128,8,128]{0,2,1:T(8,128)(2,1)}, bf16[128,8,128]{0,2,1:T(8,128)(2,1)}, u32[]{:S(2)}, u32[]{:S(2)}) collective-permute-start(bf16[128,8,128]{0,2,1:T(8,128)(2,1)} %fusion.44), channel_id=1, source_target_pairs={{1,0},{2,1},{3,2},{4,3},{5,4},{6,5},{7,6},{9,8},{10,9},{11,10},{12... | collective-permute-start | bytes 786440 | tf_op jit(solution)/shard_map/ppermute | solution.py:14
  247.8 7.5 collective-permute-start.14
  253.8 5.9 collective-permute-start.22
  256.6 6.6 collective-permute-start.15
  260.9 8.8 %collective-permute-start.23 = (bf16[128,8,128]{0,2,1:T(8,128)(2,1)S(1)}, bf16[128,8,128]{0,2,1:T(8,128)(2,1)S(1)}, u32[]{:S(2)}, u32[]{:S(2)}) collective-permute-start(bf16[128,8,128]{0,2,1:T(8,128)(2,1)S(1)} %add_convert_fusion.5), channel_id=1, source_target_pairs={{1,0},{2,1},{3,2},{4,3},{5,4},{6,5},{7,6},{9,8},{10,9},{11,10},{12... | collective-permute-start | bytes 786440 | tf_op jit(solution)/shard_map/ppermute | solution.py:14
  264.5 8.9 %collective-permute-start.16 = (bf16[8,128,128]{1,2,0:T(8,128)(2,1)S(1)}, bf16[8,128,128]{1,2,0:T(8,128)(2,1)S(1)}, u32[]{:S(2)}, u32[]{:S(2)}) collective-permute-start(bf16[8,128,128]{1,2,0:T(8,128)(2,1)S(1)} %fusion.38), channel_id=1, source_target_pairs={{1,0},{2,1},{3,2},{4,3},{5,4},{6,5},{7,6},{9,8},{10,9},{11,10},{12... | collective-permute-start | bytes 786440 | tf_op jit(solution)/shard_map/ppermute | solution.py:14
  270.8 8.3 collective-permute-start.24
  273.7 8.8 %collective-permute-start.17 = (bf16[8,128,128]{1,2,0:T(8,128)(2,1)S(1)}, bf16[8,128,128]{1,2,0:T(8,128)(2,1)S(1)}, u32[]{:S(2)}, u32[]{:S(2)}) collective-permute-start(bf16[8,128,128]{1,2,0:T(8,128)(2,1)S(1)} %fusion.39), channel_id=1, source_target_pairs={{1,0},{2,1},{3,2},{4,3},{5,4},{6,5},{7,6},{9,8},{10,9},{11,10},{12... | collective-permute-start | bytes 786440 | tf_op jit(solution)/shard_map/ppermute | solution.py:14
  280.2 7.8 collective-permute-start.25
  283.8 9.3 %collective-permute-start.18 = (bf16[8,128,128]{1,2,0:T(8,128)(2,1)S(1)}, bf16[8,128,128]{1,2,0:T(8,128)(2,1)S(1)}, u32[]{:S(2)}, u32[]{:S(2)}) collective-permute-start(bf16[8,128,128]{1,2,0:T(8,128)(2,1)S(1)} %fusion.40), channel_id=1, source_target_pairs={{1,0},{2,1},{3,2},{4,3},{5,4},{6,5},{7,6},{9,8},{10,9},{11,10},{12... | collective-permute-start | bytes 786440 | tf_op jit(solution)/shard_map/ppermute | solution.py:14
  289.1 7.8 collective-permute-start.26
  294.5 9.3 %collective-permute-start.19 = (bf16[8,128,128]{1,2,0:T(8,128)(2,1)S(1)}, bf16[8,128,128]{1,2,0:T(8,128)(2,1)S(1)}, u32[]{:S(2)}, u32[]{:S(2)}) collective-permute-start(bf16[8,128,128]{1,2,0:T(8,128)(2,1)S(1)} %fusion.41), channel_id=1, source_target_pairs={{1,0},{2,1},{3,2},{4,3},{5,4},{6,5},{7,6},{9,8},{10,9},{11,10},{12... | collective-permute-start | bytes 786440 | tf_op jit(solution)/shard_map/ppermute | solution.py:14
  297.0 18.2 %collective-permute-start.27 = (bf16[128,8,128]{0,2,1:T(8,128)(2,1)S(1)}, bf16[128,8,128]{0,2,1:T(8,128)(2,1)S(1)}, u32[]{:S(2)}, u32[]{:S(2)}) collective-permute-start(bf16[128,8,128]{0,2,1:T(8,128)(2,1)S(1)} %add_convert_fusion.1), channel_id=1, source_target_pairs={{1,0},{2,1},{3,2},{4,3},{5,4},{6,5},{7,6},{9,8},{10,9},{11,10},{12... | collective-permute-start | bytes 786440 | tf_op jit(solution)/shard_map/ppermute | solution.py:14
  304.7 11.4 %collective-permute-start.20 = (bf16[8,128,128]{1,2,0:T(8,128)(2,1)}, bf16[8,128,128]{1,2,0:T(8,128)(2,1)S(1)}, u32[]{:S(2)}, u32[]{:S(2)}) collective-permute-start(bf16[8,128,128]{1,2,0:T(8,128)(2,1)} %fusion.42), channel_id=1, source_target_pairs={{1,0},{2,1},{3,2},{4,3},{5,4},{6,5},{7,6},{9,8},{10,9},{11,10},{12... | collective-permute-start | bytes 786440 | tf_op jit(solution)/shard_map/ppermute | solution.py:14
  324.4 531.0 %copy-start.1 = (bf16[1,128,4096]{2,1,0:T(8,128)(2,1)S(1)}, bf16[1,128,4096]{2,1,0:T(8,128)(2,1)}, u32[]{:S(2)}) copy-start(bf16[1,128,4096]{2,1,0:T(8,128)(2,1)} %param.18) | copy-start | bytes 3145732
  (60 other events, 1265.1 us)
Sparse Core Ops, SparseCore 0:
  186.8 668.5 reduce-scatter.1
where the time goes:
time: 874 us; the launch traced here: 863 us
  waiting for transfers between devices  537 us (61%)
  matrix products  128 us (15%)
  other arithmetic  90.2 us (10%)
  starting transfers between devices  67.3 us (8%)
  local copies, waits for them, and re-layouts  24.1 us (3%)
  between operations  16.3 us (2%)
    reduce_scatter x1, waiting for transfers between devices, per_device(): lax.psum_scatter(lax.dot_general(out_half, dense_grad, (((0,), (0,)), (()...  515 us
    another operation x5, other arithmetic, block_parts(): jax.scipy.linalg.solve_triangular(unit, right, lower=True, unit_diagonal=...  80.4 us
    ppermute x28, starting transfers between devices, passed_along(): lax.ppermute(value, axis, [(source, source + steps) for source in range(l...  67.2 us
    ppermute x28, waiting for transfers between devices, passed_along(): lax.ppermute(value, axis, [(source, source + steps) for source in range(l...  21.8 us
  transfers between devices with their start and end apart: 29, of which 11 were waited for; matrix products, arithmetic and copies ran while one was open for 27% of the time, Pallas kernels for 0%

commit v1 on v0

v1 whole, which is shorter than its diff:
```python
import functools

import jax
import jax.numpy as jnp
from jax import lax
from jax.experimental import pallas as pl
from jax.experimental.pallas import tpu as pltpu
from jax.sharding import PartitionSpec as P

f32, bf16 = jnp.float32, jnp.bfloat16
MESH = pl.DeviceIdType.MESH
N = 128
B = 8
TOKENS = N * B
WIDTH = 4096
SLICE = WIDTH // B
HALF = SLICE // 2
ROWS = 64
SCALE = N**-0.5
GROUP = 4
Q, K, U, V, DO = range(5)


def dot(a, b, ca, cb):
    return lax.dot_general(
        a.astype(bf16), b.astype(bf16), (((ca,), (cb,)), ((), ())), preferred_element_type=f32
    )


def nn(a, b):
    return dot(a, b, 1, 0)


def nt(a, b):
    return dot(a, b, 1, 1)


def tn(a, b):
    return dot(a, b, 0, 0)


def down(*parts):
    return jnp.concatenate(parts, 0)


def beside(*parts):
    return jnp.concatenate(parts, 1)


def split(x):
    high = x.astype(bf16)
    return high, (x - high.astype(f32)).astype(bf16)


def nn3(a, b):
    ah, al = split(a)
    bh, bl = split(b)
    return nn(beside(ah, al), down(bh, bh)) + nn(ah, bl)


def masks():
    row = lax.broadcasted_iota(jnp.int32, (N, N), 0)
    col = lax.broadcasted_iota(jnp.int32, (N, N), 1)
    return row, col, row == col, row > col, col <= row


def block_forward(query, keys, raw, logit):
    row, col, eye, before, within = masks()
    prods = nt(down(raw, query), down(raw, keys))
    yield
    uu, uk, qu, qk = prods[:N, :N], prods[:N, N:], prods[N:, :N], prods[N:, N:]
    diag = jnp.where(eye, uu, 0.0)
    r_row = lax.rsqrt(jnp.sum(diag, 0, keepdims=True) + 1e-6)
    r_col = lax.rsqrt(jnp.sum(diag, 1, keepdims=True) + 1e-6)
    b_row = 2.0 / (1.0 + jnp.exp(-logit))
    b_col = jnp.sum(jnp.where(eye, b_row, 0.0), 1, keepdims=True)
    br = b_col * r_col
    lower = jnp.where(before, br * uu * r_row, 0.0)
    right = jnp.where(before, br * uk, 0.0)
    across = jnp.where(within, qu * r_row, 0.0)
    inv = jnp.where(eye, 1.0, jnp.where((row >> 1) == (col >> 1), -lower, 0.0))
    for level in range(1, 7):
        mask = ((row >> (level + 1)) == (col >> (level + 1))) & ((row >> level) != (col >> level))
        half = nn3(inv, jnp.where(mask, lower, 0.0))
        yield
        inv = inv - nn3(half, inv)
        yield
    yc = nn3(inv, beside(br * raw.astype(f32), right))
    yield
    eyc = nn3(across, yc)
    yield
    query_bar = query.astype(f32) - eyc[:, :N]
    inner = qk - eyc[:, N:]
    high, low = split(yc * r_col)
    shift = tn(down(high, low), down(raw, raw))
    move = jnp.where(eye, 1.0, 0.0) - shift[:N]
    key_tilde = keys.astype(f32) - shift[N:]
    return dict(
        uu=uu, uk=uk, r_row=r_row, r_col=r_col, b_col=b_col, across=across.astype(bf16), inv=inv.astype(bf16),
        yc=yc.astype(bf16), qhat=query_bar.astype(bf16), move=move.astype(bf16), ktil=key_tilde.astype(bf16), inner=inner,
    )


def block_backward(query, keys, raw, f, d_inner, d_qbar, d_ktil, d_move):
    row, col, eye, before, within = masks()
    r_row, r_col, b_col, yc, across = f["r_row"], f["r_col"], f["b_col"], f["yc"], f["across"]
    w = raw.astype(f32) * r_col
    wb = w.astype(bf16)
    d_in = d_inner.astype(bf16)
    d_qi = beside(d_qbar.astype(bf16), d_in)
    d_mk = down(d_move, d_ktil).astype(bf16)
    d_yc = -(tn(across, d_qi) + nt(wb, d_mk))
    yield
    d_across = jnp.where(within, -nt(d_qi, yc), 0.0).astype(bf16)
    yield
    d_br = tn(f["inv"], d_yc)
    yield
    d_lower = jnp.where(before, -nt(d_br, yc), 0.0)
    yield
    d_bw, d_right = d_br[:, :N], jnp.where(before, d_br[:, N:], 0.0)
    d_beta = jnp.sum(
        d_right * (r_col * f["uk"]) + d_lower * (r_col * f["uu"] * r_row) + d_bw * w, 1, keepdims=True
    )
    d_wk = (b_col * d_right).astype(bf16)
    d_gram = (b_col * d_lower).astype(bf16)
    kw, qw = down(keys, wb), down(query, wb)
    d_query = d_qbar + nn(beside(d_in, d_across), kw)
    yield
    d_keys = d_ktil + tn(down(d_in, d_wk), qw)
    yield
    d_w = b_col * d_bw - nn(yc, d_mk) + nn(beside(d_wk, d_gram), kw) + tn(down(d_across, d_gram), qw)
    yield
    d_raw = r_col * (d_w - w * jnp.sum(w * d_w, 1, keepdims=True))
    d_logit = d_beta * b_col * (1.0 - 0.5 * b_col)
    d_logit = jnp.sum(jnp.where(eye, d_logit, 0.0), 0, keepdims=True)
    return d_query.astype(bf16), d_keys.astype(bf16), d_raw.astype(bf16), d_logit


def together(steps):
    steps = list(steps)
    results = [None] * len(steps)
    live = list(range(len(steps)))
    while live:
        for i in list(live):
            try:
                next(steps[i])
            except StopIteration as stop:
                results[i] = stop.value
                live.remove(i)
    return results


def kernel(
    lens, q_in, k_in, v_in, u_in, l_in, proj, grad,
    dq_out, dk_out, dv_out, du_out, gp_out, dl_out,
    ins, logits, grad_own, proj_own, dout_own, grad_cut, att, made, dl_made, dl_got, prod, rs_first, mid, rs_last, fin,
    in_send, in_recv, out_send, out_recv, att_send, att_recv, rs_send, rs_recv, fin_send, fin_recv, here,
):
    dp, me = lax.axis_index("dp"), lax.axis_index("ctx")
    py, pz = lax.div(dp, 4), lax.rem(dp, 4)
    sibling = me + 1 - 2 * lax.rem(me, 2)
    peers = [lax.rem(me + o, B) for o in range(B)]
    along_y = [(lax.rem(py + o, 4), (lax.rem(py + o, 4) * 4 + pz, me)) for o in range(4)]
    along_z = [(lax.rem(pz + o, 4), (py * 4 + lax.rem(pz + o, 4), me)) for o in range(4)]
    rows = pl.ds(pl.multiple_of(me * N, N), N)

    def cols(p, width=N):
        return pl.ds(pl.multiple_of(p * width, width), width)

    sent = []

    def send(src, dst, send_sem, recv_sem, device):
        copy = pltpu.make_async_remote_copy(
            src_ref=src, dst_ref=dst, send_sem=send_sem, recv_sem=recv_sem, device_id=device, device_id_type=MESH
        )
        copy.start()
        sent.append(copy)
        return copy

    def local(src, dst, sem):
        copy = pltpu.make_async_copy(src, dst, sem)
        copy.start()
        return copy

    sources = {Q: q_in, K: k_in, U: u_in, V: v_in}
    own = [local(ref.at[0, :, cols(me)], ins.at[a, rows], here.at[a]) for a, ref in sources.items()]
    own.append(local(l_in.at[0], logits.at[me], here.at[4]))
    own_grad = local(grad.at[0], grad_own, here.at[5])
    own_cut = local(grad.at[0, :, cols(me, SLICE)], grad_cut.at[rows], here.at[6])
    own_proj = [local(proj.at[cols(peers[o])], proj_own.at[o], here.at[8 + o]) for o in range(B)]

    barrier = pltpu.get_barrier_semaphore()
    greeted = [(dp, p) for p in peers[1:]] + [d for _, d in along_y[1:]] + [d for _, d in along_z[1:]]
    for device in greeted:
        pl.semaphore_signal(barrier, inc=1, device_id=device, device_id_type=MESH)
    pl.semaphore_wait(barrier, len(greeted))

    got = {}
    for a in (U, K, Q, 5, V):
        for o in range(1, B):
            to = (dp, peers[o])
            if a == 5:
                got[a, o] = send(l_in.at[0], logits.at[me], in_send.at[a, o], in_recv.at[a, o], to)
            else:
                got[a, o] = send(
                    sources[a].at[0, :, cols(peers[o])], ins.at[a, rows], in_send.at[a, o], in_recv.at[a, o], to
                )

    own_grad.wait()
    for o in [*range(1, B), 0]:
        own_proj[o].wait()
        dout_own[o] = nt(grad_own[...], proj_own[o]).astype(bf16)
        if o:
            got[DO, o] = send(dout_own.at[o], ins.at[DO, rows], in_send.at[DO, o], in_recv.at[DO, o], (dp, peers[o]))
    own_dout = local(dout_own.at[0], ins.at[DO, rows], here.at[7])
    for o in range(1, B):
        got[6, o] = send(
            grad.at[0, :, cols(peers[o], SLICE)], grad_cut.at[rows], in_send.at[6, o], in_recv.at[6, o], (dp, peers[o])
        )

    for copy in own:
        copy.wait()
    for a in (U, K, Q, 5):
        for o in range(1, B):
            got[a, o].wait_recv()

    def block(a, c):
        return ins[a, c * N : (c + 1) * N]

    head = lax.broadcasted_iota(jnp.int32, (B, N), 0) == me
    f = []
    for g in range(0, B, GROUP):
        f += together(
            block_forward(
                block(Q, c), block(K, c), block(U, c), jnp.sum(jnp.where(head, logits[c], 0.0), 0, keepdims=True)
            )
            for c in range(g, g + GROUP)
        )
    carried = [None]
    for c in range(1, B):
        new = f[c - 1]["ktil"]
        carried.append(new if c == 1 else down(nn(carried[c - 1], f[c - 1]["move"]).astype(bf16), new))

    for o in range(1, B):
        got[V, o].wait_recv()
    ends = [lens[0, 0]]
    for i in range(1, 4):
        ends.append(ends[-1] + lens[0, i])
    probs = []
    for c in range(B):
        span = (c + 1) * N
        place = lax.broadcasted_iota(jnp.int32, (N, 1), 0) + c * N
        start = jnp.zeros((N, 1), jnp.int32)
        for end in ends:
            start = jnp.where(end <= place, jnp.maximum(start, end), start)
        key_place = lax.broadcasted_iota(jnp.int32, (N, span), 1)
        seen = (key_place >= start) & (key_place <= place)
        raw = f[c]["inner"] if c == 0 else beside(nt(f[c]["qhat"], carried[c]), f[c]["inner"])
        score = jnp.where(seen, raw * SCALE, -1e30)
        part = jnp.exp(score - jnp.max(score, 1, keepdims=True))
        prob = part / jnp.sum(part, 1, keepdims=True)
        probs.append(prob)
        att[me, c * N : (c + 1) * N] = nn(prob, ins[V, :span]).astype(bf16)

    att_got = []
    for i, o in enumerate((2, 4, 6)):
        att_got.append(send(att.at[me], att.at[me], att_send.at[i], att_recv.at[i], (dp, peers[o])))
    att_got.append(send(att.at[me], att.at[me], att_send.at[3], att_recv.at[3], (dp, sibling)))

    own_dout.wait()
    for o in range(1, B):
        got[DO, o].wait_recv()
    d_inner, d_qbar, d_carried = [], [], [None] * B
    d_value = [None] * B
    for c in range(B):
        span = (c + 1) * N
        grads = block(DO, c)
        prob = probs[c]
        d_prob = nt(grads, ins[V, :span])
        d_score = prob * (d_prob - jnp.sum(prob * d_prob, 1, keepdims=True)) * SCALE
        term = tn(prob, grads)
        for j in range(c + 1):
            piece = term[j * N : (j + 1) * N]
            d_value[j] = piece if j == c else d_value[j] + piece
        d_inner.append(d_score[:, c * N :])
        if c:
            early = d_score[:, : c * N].astype(bf16)
            d_qbar.append(nn(early, carried[c]))
            d_carried[c] = tn(early, f[c]["qhat"])
        else:
            d_qbar.append(jnp.zeros((N, N), f32))
    out = {}

    def send_made(i, result):
        out[i, 0] = local(made.at[i, rows], result.at[0, :, cols(me)], here.at[16 + i])
        for o in range(1, B):
            out[i, o] = send(
                made.at[i, cols(peers[o])], result.at[0, :, cols(me)], out_send.at[i, o], out_recv.at[i, o], (dp, peers[o])
            )

    for j in range(B):
        made[3, j * N : (j + 1) * N] = d_value[j].astype(bf16)
    send_made(3, dv_out)

    d_ktil = [None] * (B - 1) + [jnp.zeros((N, N), f32)]
    d_move = [jnp.zeros((N, N), f32)] * B
    later = None
    for c in range(B - 1, 0, -1):
        now = d_carried[c]
        if later is not None:
            back = later[: c * N].astype(bf16)
            now = now + nt(back, f[c]["move"])
            d_move[c] = tn(carried[c], back)
        d_ktil[c - 1] = now[(c - 1) * N :]
        later = now

    for i, o in enumerate((2, 4, 6)):
        att_got[i].wait_recv()
        source = lax.rem(me + B - o, B)
        att_got.append(send(att.at[source], att.at[source], att_send.at[4 + i], att_recv.at[4 + i], (dp, sibling)))

    for g in range(0, B, GROUP):
        results = together(
            block_backward(
                block(Q, c), block(K, c), block(U, c), f[c], d_inner[c], d_qbar[c], d_ktil[c], d_move[c]
            )
            for c in range(g, g + GROUP)
        )
        for c, (d_query, d_keys, d_raw, d_logit) in zip(range(g, g + GROUP), results):
            made[0, c * N : (c + 1) * N] = d_query
            made[1, c * N : (c + 1) * N] = d_keys
            made[2, c * N : (c + 1) * N] = d_raw
            dl_made[c] = jnp.where(head, d_logit, 0.0)
    send_made(0, dq_out)
    send_made(1, dk_out)
    send_made(2, du_out)
    out[4, 0] = local(dl_made.at[me], dl_got.at[me], here.at[20])
    for o in range(1, B):
        out[4, o] = send(
            dl_made.at[peers[o]], dl_got.at[me], out_send.at[4, o], out_recv.at[4, o], (dp, peers[o])
        )

    own_cut.wait()
    for o in range(1, B):
        got[6, o].wait_recv()
    for copy in att_got[3:]:
        copy.wait_recv()
    for h in range(B):
        term = tn(att[h], grad_cut[...]).astype(bf16)
        prod[h // 2, 2 * (h % 2)] = term[:ROWS]
        prod[h // 2, 2 * (h % 2) + 1] = term[ROWS:]

    left, right = pl.ds(0, HALF), pl.ds(HALF, HALF)
    first = []
    for o in range(1, 4):
        jy, dev_y = along_y[o]
        first.append(
            send(prod.at[jy, :, :, left], rs_first.at[0, o - 1], rs_send.at[0, o], rs_recv.at[0, o], dev_y)
        )
        jz, dev_z = along_z[o]
        first.append(
            send(prod.at[:, jz, :, right], rs_first.at[1, o - 1], rs_send.at[1, o], rs_recv.at[1, o], dev_z)
        )
    for copy in first:
        copy.wait_recv()
    mid[0] = (prod[py, :, :, :HALF].astype(f32) + sum(rs_first[0, i].astype(f32) for i in range(3))).astype(bf16)
    mid[1] = (prod[:, pz, :, HALF:].astype(f32) + sum(rs_first[1, i].astype(f32) for i in range(3))).astype(bf16)
    last = []
    for o in range(1, 4):
        jz, dev_z = along_z[o]
        last.append(send(mid.at[0, jz], rs_last.at[0, o - 1], rs_send.at[2, o], rs_recv.at[2, o], dev_z))
        jy, dev_y = along_y[o]
        last.append(send(mid.at[1, jy], rs_last.at[1, o - 1], rs_send.at[3, o], rs_recv.at[3, o], dev_y))
    for copy in last:
        copy.wait_recv()
    total = beside(
        mid[0, pz].astype(f32) + sum(rs_last[0, i].astype(f32) for i in range(3)),
        mid[1, py].astype(f32) + sum(rs_last[1, i].astype(f32) for i in range(3)),
    )
    for p in range(B):
        fin[p] = total[p * 8 : (p + 1) * 8]
    gp_own = local(fin.at[me], gp_out.at[:, cols(me, SLICE)], here.at[21])
    gp_got = [
        send(fin.at[peers[o]], gp_out.at[:, cols(me, SLICE)], fin_send.at[o], fin_recv.at[o], (dp, peers[o]))
        for o in range(1, B)
    ]

    for i in range(5):
        out[i, 0].wait()
        for o in range(1, B):
            out[i, o].wait_recv()
    dl_out[0] = sum(dl_got[h] for h in range(B))
    gp_own.wait()
    for copy in gp_got:
        copy.wait_recv()
    for copy in sent:
        copy.wait_send()


def per_device(queries, keys, values, directions, beta_logits, out_proj, out_grad, doc_lengths):
    tokens = jax.ShapeDtypeStruct((1, N, TOKENS), bf16)
    anywhere = pl.BlockSpec(memory_space=pl.ANY)
    dma = pltpu.SemaphoreType.DMA
    dq, dk, dv, du, gp, dl = pl.pallas_call(
        kernel,
        out_shape=[tokens] * 4
        + [jax.ShapeDtypeStruct((B, WIDTH), f32), jax.ShapeDtypeStruct((1, B, N), f32)],
        in_specs=[pl.BlockSpec(memory_space=pltpu.SMEM)] + [anywhere] * 7,
        out_specs=[anywhere] * 5 + [pl.BlockSpec(memory_space=pltpu.VMEM)],
        scratch_shapes=[
            pltpu.VMEM((5, TOKENS, N), bf16),
            pltpu.VMEM((B, B, N), f32),
            pltpu.VMEM((N, WIDTH), bf16),
            pltpu.VMEM((B, N, WIDTH), bf16),
            pltpu.VMEM((B, N, N), bf16),
            pltpu.VMEM((TOKENS, SLICE), bf16),
            pltpu.VMEM((B, TOKENS, N), bf16),
            pltpu.VMEM((4, TOKENS, N), bf16),
            pltpu.VMEM((B, B, N), f32),
            pltpu.VMEM((B, B, N), f32),
            pltpu.VMEM((4, 4, ROWS, SLICE), bf16),
            pltpu.VMEM((2, 3, 4, ROWS, HALF), bf16),
            pltpu.VMEM((2, 4, ROWS, HALF), bf16),
            pltpu.VMEM((2, 3, ROWS, HALF), bf16),
            pltpu.VMEM((B, B, SLICE), f32),
            dma((7, B)),
            dma((7, B)),
            dma((5, B)),
            dma((5, B)),
            dma((7,)),
            dma((7,)),
            dma((4, 4)),
            dma((4, 4)),
            dma((B,)),
            dma((B,)),
            dma((22,)),
        ],
        compiler_params=pltpu.CompilerParams(
            collective_id=0, has_side_effects=True, vmem_limit_bytes=56 * 2**20
        ),
    )(doc_lengths, queries, keys, values, directions, beta_logits, out_proj, out_grad)
    return dq, dk, dv, du, dl, gp


def solution(mesh):
    rows = P("dp", "ctx", None)
    return jax.shard_map(
        per_device,
        mesh=mesh,
        in_specs=(rows, rows, rows, rows, P("dp", None, "ctx"), P(), rows, P("dp", None)),
        out_specs=(rows, rows, rows, rows, P("dp", None, "ctx"), P(("dp", "ctx"), None)),
        check_vma=False,
    )
```

time: 874 us -> 82.3 us (0.09)
  the two profiles are of different devices: /device:TPU:0 before, /device:TPU:1 now
where the time goes in v1:
time: 82.3 us; the launch traced here: 82 us
  Pallas kernels  71.8 us (87%)
  local copies, waits for them, and re-layouts  9.51 us (12%)
    pallas_call x1, Pallas kernels, per_device(): pl.pallas_call(kernel, out_shape=[tokens] * 4 + [jax.ShapeDtypeStruct((B,...  71.8 us
    unnamed x6, local copies, waits for them, and re-layouts  9.51 us

profile of v1, /device:TPU:1, one launch (start us, length us, event | category | flops | bytes accessed | tf_op | source)
XLA Modules:
  0.0 82.0 jit_solution(4019863129680790722)
XLA Ops:
  0.6 71.8 %shard_map.127 = (bf16[1,128,1024]{2,1,0:T(8,128)(2,1)}, bf16[1,128,1024]{2,1,0:T(8,128)(2,1)}, bf16[1,128,1024]{2,1,0:T(8,128)(2,1)}, bf16[1,128,1024]{2,1,0:T(...) custom-call(s32[1,4]{1,0:T(1,128)} %lens.1, bf16[1,128,1024]{2,1,0:T(8,128)(2,1)} %q_in.1, ...), custom_call_target="tpu_custom_call" | custom-call | tf_op jit(solution)/shard_map/pallas_call | solution.py:404
  72.5 1.7 %copy.20 = bf16[1,128,1024]{2,1,0:T(8,128)(2,1)} copy(bf16[1,128,1024]{2,1,0:T(8,128)(2,1)} %get-tuple-element.24) | data formatting | bytes 524288
  74.2 1.7 %copy.21 = bf16[1,128,1024]{2,1,0:T(8,128)(2,1)} copy(bf16[1,128,1024]{2,1,0:T(8,128)(2,1)} %get-tuple-element.25) | data formatting | bytes 524288
  75.8 1.7 %copy.22 = bf16[1,128,1024]{2,1,0:T(8,128)(2,1)} copy(bf16[1,128,1024]{2,1,0:T(8,128)(2,1)} %get-tuple-element.26) | data formatting | bytes 524288
  77.5 1.7 %copy.23 = bf16[1,128,1024]{2,1,0:T(8,128)(2,1)} copy(bf16[1,128,1024]{2,1,0:T(8,128)(2,1)} %get-tuple-element.27) | data formatting | bytes 524288
  79.2 1.3 %copy.24 = f32[1,8,128]{2,1,0:T(8,128)} copy(f32[1,8,128]{2,1,0:T(8,128)} %get-tuple-element.28) | data formatting | bytes 8192
  80.4 1.6 %copy.25 = f32[8,4096]{1,0:T(8,128)} copy(f32[8,4096]{1,0:T(8,128)} %get-tuple-element.29) | data formatting | bytes 262144

commit v2 on v1

v2 whole, which is shorter than its diff:
```python
import functools

import jax
import jax.numpy as jnp
from jax import lax
from jax.experimental import pallas as pl
from jax.experimental.pallas import tpu as pltpu
from jax.sharding import PartitionSpec as P

f32, bf16 = jnp.float32, jnp.bfloat16
MESH = pl.DeviceIdType.MESH
N = 128
B = 8
TOKENS = N * B
WIDTH = 4096
PART = WIDTH // 4
SCALE = N**-0.5
Q, K, U, V, DO = range(5)
FIELDS = {
    "uu": ((N, N), f32), "uk": ((N, N), f32), "inner": ((N, N), f32), "r_row": ((1, N), f32), "r_col": ((N, 1), f32),
    "b_col": ((N, 1), f32), "across": ((N, N), bf16), "inv": ((N, N), bf16), "yc": ((N, 2 * N), bf16),
    "qhat": ((N, N), bf16), "move": ((N, N), bf16), "ktil": ((N, N), bf16), "d_inner": ((N, N), bf16),
    "d_qbar": ((N, N), f32), "d_ktil": ((N, N), f32), "d_move": ((N, N), bf16),
}
NEAR, NEXT, FAR = (1,), (2, 3, 6, 7), (4, 5)


def dot(a, b, ca, cb):
    return lax.dot_general(
        a.astype(bf16), b.astype(bf16), (((ca,), (cb,)), ((), ())), preferred_element_type=f32
    )


def nn(a, b):
    return dot(a, b, 1, 0)


def nt(a, b):
    return dot(a, b, 1, 1)


def tn(a, b):
    return dot(a, b, 0, 0)


def down(*parts):
    return jnp.concatenate(parts, 0)


def beside(*parts):
    return jnp.concatenate(parts, 1)


def split(x):
    high = x.astype(bf16)
    return high, (x - high.astype(f32)).astype(bf16)


def nn3(a, b):
    ah, al = split(a)
    bh, bl = split(b)
    return nn(beside(ah, al), down(bh, bh)) + nn(ah, bl)


def masks():
    row = lax.broadcasted_iota(jnp.int32, (N, N), 0)
    col = lax.broadcasted_iota(jnp.int32, (N, N), 1)
    return row, col, row == col, row > col, col <= row


def block_forward(c, ins, logit, f):
    query, keys, raw = (ins[a, pl.ds(c * N, N)] for a in (Q, K, U))
    row, col, eye, before, within = masks()
    prods = nt(down(raw, query), down(raw, keys))
    yield
    uu, uk, qu, qk = prods[:N, :N], prods[:N, N:], prods[N:, :N], prods[N:, N:]
    diag = jnp.where(eye, uu, 0.0)
    r_row = lax.rsqrt(jnp.sum(diag, 0, keepdims=True) + 1e-6)
    r_col = lax.rsqrt(jnp.sum(diag, 1, keepdims=True) + 1e-6)
    b_row = 2.0 / (1.0 + jnp.exp(-logit))
    b_col = jnp.sum(jnp.where(eye, b_row, 0.0), 1, keepdims=True)
    br = b_col * r_col
    lower = jnp.where(before, br * uu * r_row, 0.0)
    right = jnp.where(before, br * uk, 0.0)
    across = jnp.where(within, qu * r_row, 0.0)
    inv = jnp.where(eye, 1.0, jnp.where((row >> 1) == (col >> 1), -lower, 0.0))
    for level in range(1, 7):
        mask = ((row >> (level + 1)) == (col >> (level + 1))) & ((row >> level) != (col >> level))
        half = nn3(inv, jnp.where(mask, lower, 0.0))
        yield
        inv = inv - nn3(half, inv)
        yield
    yc = nn3(inv, beside(br * raw.astype(f32), right))
    yield
    eyc = nn3(across, yc)
    yield
    query_bar = query.astype(f32) - eyc[:, :N]
    inner = qk - eyc[:, N:]
    high, low = split(yc * r_col)
    shift = tn(down(high, low), down(raw, raw))
    move = jnp.where(eye, 1.0, 0.0) - shift[:N]
    key_tilde = keys.astype(f32) - shift[N:]
    f["uu"][c], f["uk"][c], f["r_row"][c], f["r_col"][c], f["b_col"][c] = uu, uk, r_row, r_col, b_col
    f["across"][c], f["inv"][c], f["yc"][c] = across.astype(bf16), inv.astype(bf16), yc.astype(bf16)
    f["qhat"][c], f["move"][c], f["ktil"][c] = query_bar.astype(bf16), move.astype(bf16), key_tilde.astype(bf16)
    f["inner"][c] = inner


def block_backward(c, ins, f):
    query, keys, raw = (ins[a, pl.ds(c * N, N)] for a in (Q, K, U))
    row, col, eye, before, within = masks()
    r_row, r_col, b_col, yc, across = (f[name][c] for name in ("r_row", "r_col", "b_col", "yc", "across"))
    d_in, d_qbar, d_ktil = f["d_inner"][c], f["d_qbar"][c], f["d_ktil"][c]
    w = raw.astype(f32) * r_col
    wb = w.astype(bf16)
    d_qi = beside(d_qbar.astype(bf16), d_in)
    d_mk = down(f["d_move"][c], d_ktil.astype(bf16))
    d_yc = -(tn(across, d_qi) + nt(wb, d_mk))
    yield
    d_across = jnp.where(within, -nt(d_qi, yc), 0.0).astype(bf16)
    yield
    d_br = tn(f["inv"][c], d_yc)
    yield
    d_lower = jnp.where(before, -nt(d_br, yc), 0.0)
    yield
    d_bw, d_right = d_br[:, :N], jnp.where(before, d_br[:, N:], 0.0)
    d_beta = jnp.sum(
        d_right * (r_col * f["uk"][c]) + d_lower * (r_col * f["uu"][c] * r_row) + d_bw * w, 1, keepdims=True
    )
    d_wk = (b_col * d_right).astype(bf16)
    d_gram = (b_col * d_lower).astype(bf16)
    kw, qw = down(keys, wb), down(query, wb)
    d_query = d_qbar + nn(beside(d_in, d_across), kw)
    yield
    d_keys = d_ktil + tn(down(d_in, d_wk), qw)
    yield
    d_w = b_col * d_bw - nn(yc, d_mk) + nn(beside(d_wk, d_gram), kw) + tn(down(d_across, d_gram), qw)
    yield
    d_raw = r_col * (d_w - w * jnp.sum(w * d_w, 1, keepdims=True))
    d_logit = d_beta * b_col * (1.0 - 0.5 * b_col)
    d_logit = jnp.sum(jnp.where(eye, d_logit, 0.0), 0, keepdims=True)
    return d_query.astype(bf16), d_keys.astype(bf16), d_raw.astype(bf16), d_logit


def together(steps):
    steps = list(steps)
    results = [None] * len(steps)
    live = list(range(len(steps)))
    while live:
        for i in list(live):
            try:
                next(steps[i])
            except StopIteration as stop:
                results[i] = stop.value
                live.remove(i)
    return results


def kernel(
    lens, q_in, k_in, v_in, u_in, l_in, proj, grad,
    dq_out, dk_out, dv_out, du_out, gp_out, dl_out,
    ins, logits, grad_own, proj_own, dout_own, grad_z, grad_y, att_own, att, att_z, att_y, made, dl_made, dl_got, prod, rs_first, mid, rs_last, fin,
    in_send, in_recv, out_send, out_recv, att_send, att_recv, rs_send, rs_recv, fin_send, fin_recv, here, *parts,
):
    f = dict(zip(FIELDS, parts))
    dp, me = lax.axis_index("dp"), lax.axis_index("ctx")
    py, pz = lax.div(dp, 4), lax.rem(dp, 4)
    sibling = me + 1 - 2 * lax.rem(me, 2)
    px, core = lax.div(me, 2), lax.rem(me, 2)
    y_at = [lax.rem(py + o, 4) for o in range(4)]
    z_at = [lax.rem(pz + o, 4) for o in range(4)]
    x_at = [lax.rem(px + o, 4) for o in range(4)]
    peers = [x_at[o // 2] * 2 + lax.rem(core + o % 2, 2) for o in range(B)]
    along_y = [(y * 4 + pz, me) for y in y_at]
    along_z = [(py * 4 + z, me) for z in z_at]
    along_x = [(dp, x * 2 + core) for x in x_at]
    z_slot, y_slot = pz * 2 + core, py * 2 + core
    z_group = [(c, (py * 4 + z, px * 2 + c), z) for z in z_at for c in (core, 1 - core)]
    y_group = [(c, (y * 4 + pz, px * 2 + c), y) for y in y_at for c in (core, 1 - core)]
    rows = pl.ds(pl.multiple_of(me * N, N), N)

    def cols(p, width=N):
        return pl.ds(pl.multiple_of(p * width, width), width)

    sent = []

    def send(src, dst, send_sem, recv_sem, device):
        copy = pltpu.make_async_remote_copy(
            src_ref=src, dst_ref=dst, send_sem=send_sem, recv_sem=recv_sem, device_id=device, device_id_type=MESH
        )
        copy.start()
        sent.append(copy)
        return copy

    def local(src, dst, sem):
        copy = pltpu.make_async_copy(src, dst, sem)
        copy.start()
        return copy

    sources = {Q: q_in, K: k_in, U: u_in, V: v_in}
    own = [local(ref.at[0, :, cols(me)], ins.at[a, rows], here.at[a]) for a, ref in sources.items()]
    own.append(local(l_in.at[0], logits.at[me], here.at[4]))
    own_grad = local(grad.at[0], grad_own, here.at[5])
    z_rows, y_rows = (pl.ds(pl.multiple_of(slot * N, N), N) for slot in (z_slot, y_slot))
    own_cut = [
        local(grad.at[0, :, cols(core, PART)], grad_z.at[z_rows], here.at[6]),
        local(grad.at[0, :, cols(core + 2, PART)], grad_y.at[y_rows], here.at[22]),
    ]
    own_proj = [local(proj.at[cols(x_at[dx], 2 * N)], proj_own.at[dx], here.at[8 + dx]) for dx in range(4)]

    barrier = pltpu.get_barrier_semaphore()
    greeted = [(dp, p) for p in peers[1:]] + [d for _, d, _ in y_group[2:] + z_group[2:]]
    for device in greeted:
        pl.semaphore_signal(barrier, inc=1, device_id=device, device_id_type=MESH)
    pl.semaphore_wait(barrier, len(greeted))

    got = {}

    def send_in(a, o):
        if a == 5:
            src, dst = l_in.at[0], logits.at[me]
        else:
            src, dst = sources[a].at[0, :, cols(peers[o])], ins.at[a, rows]
        got[a, o] = send(src, dst, in_send.at[a, o], in_recv.at[a, o], (dp, peers[o]))

    for near in (NEAR, NEXT, FAR):
        for a in (U, K, Q, 5):
            for o in near:
                send_in(a, o)
    for o in (*NEXT, *FAR, *NEAR):
        send_in(V, o)

    for o in range(1, B):
        c, to, _ = z_group[o]
        got[6, o] = send(grad.at[0, :, cols(c, PART)], grad_z.at[z_rows], in_send.at[6, o], in_recv.at[6, o], to)
        c, to, _ = y_group[o]
        got[7, o] = send(grad.at[0, :, cols(c + 2, PART)], grad_y.at[y_rows], in_send.at[7, o], in_recv.at[7, o], to)

    for copy in own:
        copy.wait()
    head = lax.broadcasted_iota(jnp.int32, (B, N), 0) == me

    def forward_of(blocks, arrivals):
        for a in (U, K, Q, 5):
            for o in arrivals:
                got[a, o].wait_recv()
        own_logits = [jnp.sum(jnp.where(head, logits[c], 0.0), 0, keepdims=True) for c in blocks]
        together(block_forward(c, ins, logit, f) for c, logit in zip(blocks, own_logits))

    forward_of([peers[o] for o in (0, 1)], NEAR)

    own_grad.wait()
    for dx in (1, 3, 2, 0):
        own_proj[dx].wait()
        both = nt(grad_own[...], proj_own[dx]).astype(bf16)
        for c in range(2):
            dout_own[dx, c] = both[:, c * N : (c + 1) * N]
        for o in (2 * dx, 2 * dx + 1):
            if o:
                src = dout_own.at[dx, lax.rem(peers[o], 2)]
                got[DO, o] = send(src, ins.at[DO, rows], in_send.at[DO, o], in_recv.at[DO, o], (dp, peers[o]))
    own_dout = local(dout_own.at[0, core], ins.at[DO, rows], here.at[7])

    forward_of([peers[o] for o in NEXT + FAR], NEXT + FAR)

    def block(a, c):
        return ins[a, c * N : (c + 1) * N]

    for o in range(1, B):
        got[V, o].wait_recv()
    ends = [lens[0, 0]]
    for i in range(1, 4):
        ends.append(ends[-1] + lens[0, i])
    carried, probs = [None] * B, [None] * B

    def carry_on():
        for c in range(1, B):
            new = f["ktil"][c - 1]
            carried[c] = new if c == 1 else down(nn(carried[c - 1], f["move"][c - 1]).astype(bf16), new)
            yield

    def row_forward(c):
        for _ in range(c):
            yield
        span = (c + 1) * N
        place = lax.broadcasted_iota(jnp.int32, (N, 1), 0) + c * N
        start = jnp.zeros((N, 1), jnp.int32)
        for end in ends:
            start = jnp.where(end <= place, jnp.maximum(start, end), start)
        key_place = lax.broadcasted_iota(jnp.int32, (N, span), 1)
        seen = (key_place >= start) & (key_place <= place)
        raw = f["inner"][c] if c == 0 else beside(nt(f["qhat"][c], carried[c]), f["inner"][c])
        yield
        score = jnp.where(seen, raw * SCALE, -1e30)
        peak = jnp.max(score, 1, keepdims=True)
        yield
        part = jnp.exp(score - peak)
        mass = jnp.sum(part, 1, keepdims=True)
        yield
        probs[c] = part * (1.0 / mass)
        result = nn(probs[c], ins[V, :span])
        yield
        att_own[c] = result.T.astype(bf16).reshape(2, 64, N)

    together([carry_on(), *(row_forward(c) for c in range(B))])

    own_att = local(att_own.at[me], att.at[lax.div(me, 2), pl.ds(lax.rem(me, 2) * 2, 2)], here.at[23])
    att_got = []
    for o in range(1, B):
        att_got.append(
            send(
                att_own.at[peers[o]], att.at[lax.div(me, 2), pl.ds(lax.rem(me, 2) * 2, 2)],
                att_send.at[0, o], att_recv.at[0, o], (dp, peers[o]),
            )
        )

    own_dout.wait()
    for o in range(1, B):
        got[DO, o].wait_recv()
    d_carried, d_value = [None] * B, [None] * B

    def row_backward(c):
        for _ in range(B - 1 - c):
            yield
        span = (c + 1) * N
        grads, prob = block(DO, c), probs[c]
        d_prob = nt(grads, ins[V, :span])
        yield
        mean = jnp.sum(prob * d_prob, 1, keepdims=True)
        yield
        d_score = prob * (d_prob - mean) * SCALE
        f["d_inner"][c] = d_score[:, c * N :].astype(bf16)
        if c:
            early = d_score[:, : c * N].astype(bf16)
            d_carried[c] = tn(early, f["qhat"][c])
            yield
            f["d_qbar"][c] = nn(early, carried[c])
        else:
            f["d_qbar"][c] = jnp.zeros((N, N), f32)
        yield
        term = tn(prob, grads)
        for j in range(c + 1):
            piece = term[j * N : (j + 1) * N]
            d_value[j] = piece if d_value[j] is None else d_value[j] + piece

    def carry_back():
        f["d_ktil"][B - 1] = jnp.zeros((N, N), f32)
        for c in (0, B - 1):
            f["d_move"][c] = jnp.zeros((N, N), bf16)
        later = None
        for c in range(B - 1, 0, -1):
            while d_carried[c] is None:
                yield
            now = d_carried[c]
            if later is not None:
                back = later[: c * N].astype(bf16)
                now = now + nt(back, f["move"][c])
                f["d_move"][c] = tn(carried[c], back).astype(bf16)
            f["d_ktil"][c - 1] = now[(c - 1) * N :]
            later = now
            yield

    together([*(row_backward(c) for c in range(B - 1, -1, -1)), carry_back()])

    out = {}
    results = (dq_out, dk_out, du_out, dv_out)

    def send_out(i, o):
        src, dst = made.at[i, cols(peers[o])], results[i].at[0, :, cols(me)]
        if o:
            out[i, o] = send(src, dst, out_send.at[i, o], out_recv.at[i, o], (dp, peers[o]))
        else:
            out[i, o] = local(src, dst, here.at[16 + i])

    for j in range(B):
        made[3, j * N : (j + 1) * N] = d_value[j].astype(bf16)
    for o in (*NEXT, *FAR, *NEAR, 0):
        send_out(3, o)

    own_att.wait()
    for copy in att_got:
        copy.wait_recv()
    own_share = [
        local(att.at[:, pz], att_z.at[z_slot], here.at[24]),
        local(att.at[py], att_y.at[y_slot], here.at[25]),
    ]
    shared = []
    for o in range(1, B):
        _, to, z = z_group[o]
        shared.append(send(att.at[:, z], att_z.at[z_slot], att_send.at[1, o], att_recv.at[1, o], to))
        _, to, y = y_group[o]
        shared.append(send(att.at[y], att_y.at[y_slot], att_send.at[2, o], att_recv.at[2, o], to))

    for some in (NEXT, FAR + (1, 0)):
        blocks = [peers[o] for o in some]
        for o, c, result in zip(some, blocks, together(block_backward(c, ins, f) for c in blocks)):
            for i in range(3):
                made[i, cols(c)] = result[i]
            dl_made[c] = jnp.where(head, result[3], 0.0)
            for i in range(3):
                send_out(i, o)
            if o:
                out[4, o] = send(dl_made.at[c], dl_got.at[me], out_send.at[4, o], out_recv.at[4, o], (dp, c))
            else:
                out[4, o] = local(dl_made.at[c], dl_got.at[me], here.at[20])

    for copy in own_cut + own_share:
        copy.wait()
    for o in range(1, B):
        got[6, o].wait_recv()
        got[7, o].wait_recv()
    for copy in shared:
        copy.wait_recv()
    for i, (left, right) in enumerate(((att_z, grad_z), (att_y, grad_y))):
        rows_of = beside(*(left[m].reshape(2 * N, N) for m in range(B)))
        prod[i] = nn(rows_of, right[...]).astype(bf16).reshape(4, 64, PART)

    first = []
    for o in range(1, 4):
        first.append(send(prod.at[0, y_at[o]], rs_first.at[0, o - 1], rs_send.at[0, o], rs_recv.at[0, o], along_y[o]))
        first.append(send(prod.at[1, z_at[o]], rs_first.at[1, o - 1], rs_send.at[1, o], rs_recv.at[1, o], along_z[o]))
    for copy in first:
        copy.wait_recv()
    for i, own in enumerate((py, pz)):
        part = prod[i, own].astype(f32) + sum(rs_first[i, o].astype(f32) for o in range(3))
        mid[:, i] = part.astype(bf16).reshape(4, 16, PART)
    last = []
    for o in range(1, 4):
        last.append(send(mid.at[x_at[o]], rs_last.at[o - 1], rs_send.at[2, o], rs_recv.at[2, o], along_x[o]))
    for copy in last:
        copy.wait_recv()
    total = mid[px].astype(f32) + sum(rs_last[o].astype(f32) for o in range(3))
    for c in range(2):
        fin[c] = total[:, c * 8 : c * 8 + 8]
    gp_own, gp_got = [], []
    for i in range(2):
        place = cols(core + 2 * i, PART)
        gp_own.append(local(fin.at[core, i], gp_out.at[:, place], here.at[26 + i]))
        gp_got.append(
            send(fin.at[1 - core, i], gp_out.at[:, place], fin_send.at[i], fin_recv.at[i], (dp, sibling))
        )

    for i in range(5):
        out[i, 0].wait()
        for o in range(1, B):
            out[i, o].wait_recv()
    dl_out[0] = sum(dl_got[h] for h in range(B))
    for copy in gp_own:
        copy.wait()
    for copy in gp_got:
        copy.wait_recv()
    for copy in sent:
        copy.wait_send()


def hand_over(*refs):
    count = (len(refs) - 1) // 2
    sems = refs[-1]
    copies = [pltpu.make_async_copy(refs[i], refs[count + i], sems.at[i]) for i in range(count)]
    for copy in copies:
        copy.start()
    for copy in copies:
        copy.wait()


def per_device(queries, keys, values, directions, beta_logits, out_proj, out_grad, doc_lengths):
    tokens = jax.ShapeDtypeStruct((1, N, TOKENS), bf16)
    anywhere = pl.BlockSpec(memory_space=pl.ANY)
    dma = pltpu.SemaphoreType.DMA
    results = [tokens] * 4 + [jax.ShapeDtypeStruct((B, WIDTH), f32), jax.ShapeDtypeStruct((1, B, N), f32)]
    made = pl.pallas_call(
        kernel,
        out_shape=results,
        in_specs=[pl.BlockSpec(memory_space=pltpu.SMEM)] + [anywhere] * 7,
        out_specs=[anywhere] * 5 + [pl.BlockSpec(memory_space=pltpu.VMEM)],
        scratch_shapes=[
            pltpu.VMEM((5, TOKENS, N), bf16),
            pltpu.VMEM((B, B, N), f32),
            pltpu.VMEM((N, WIDTH), bf16),
            pltpu.VMEM((4, 2 * N, WIDTH), bf16),
            pltpu.VMEM((4, 2, N, N), bf16),
            pltpu.VMEM((TOKENS, PART), bf16),
            pltpu.VMEM((TOKENS, PART), bf16),
            pltpu.VMEM((B, 2, 64, N), bf16),
            pltpu.VMEM((4, 4, 64, N), bf16),
            pltpu.VMEM((B, 4, 64, N), bf16),
            pltpu.VMEM((B, 4, 64, N), bf16),
            pltpu.VMEM((4, TOKENS, N), bf16),
            pltpu.VMEM((B, B, N), f32),
            pltpu.VMEM((B, B, N), f32),
            pltpu.VMEM((2, 4, 64, PART), bf16),
            pltpu.VMEM((2, 3, 64, PART), bf16),
            pltpu.VMEM((4, 2, 16, PART), bf16),
            pltpu.VMEM((3, 2, 16, PART), bf16),
            pltpu.VMEM((2, 2, 8, PART), f32),
            dma((8, B)),
            dma((8, B)),
            dma((5, B)),
            dma((5, B)),
            dma((3, B)),
            dma((3, B)),
            dma((4, 4)),
            dma((4, 4)),
            dma((2,)),
            dma((2,)),
            dma((28,)),
            *(pltpu.VMEM((B, *shape), dtype) for shape, dtype in FIELDS.values()),
        ],
        compiler_params=pltpu.CompilerParams(
            collective_id=0, has_side_effects=True, vmem_limit_bytes=56 * 2**20
        ),
    )(doc_lengths, queries, keys, values, directions, beta_logits, out_proj, out_grad)
    dq, dk, dv, du, gp, dl = pl.pallas_call(
        hand_over,
        out_shape=results,
        in_specs=[anywhere] * 6,
        out_specs=[pl.BlockSpec(memory_space=pltpu.VMEM)] * 6,
        scratch_shapes=[dma((6,))],
    )(*made)
    return dq, dk, dv, du, dl, gp


def solution(mesh):
    rows = P("dp", "ctx", None)
    return jax.shard_map(
        per_device,
        mesh=mesh,
        in_specs=(rows, rows, rows, rows, P("dp", None, "ctx"), P(), rows, P("dp", None)),
        out_specs=(rows, rows, rows, rows, P("dp", None, "ctx"), P(("dp", "ctx"), None)),
        check_vma=False,
    )
```

time: 82.3 us -> 63 us (0.77)
  Pallas kernels: 71.8 us -> 62.1 us
  local copies, waits for them, and re-layouts: 9.51 us -> 0 us
    pallas_call x1 -> x2, Pallas kernels: 71.8 us -> 62.1 us  [the longest x1 59.8 us: per_device(): pl.pallas_call(kernel, out_shape=results, in_specs=[pl.BlockSpec(memory_s...]
    unnamed x6 -> x0, local copies, waits for them, and re-layouts: 9.51 us -> none
where the time goes in v2:
time: 63 us; the launch traced here: 62.9 us
  Pallas kernels  62.1 us (99%)
  between operations  0.8 us (1%)
    pallas_call x1, Pallas kernels, per_device(): pl.pallas_call(kernel, out_shape=results, in_specs=[pl.BlockSpec(memory_s...  59.8 us
    pallas_call x1, Pallas kernels, per_device(): pl.pallas_call(hand_over, out_shape=results, in_specs=[anywhere] * 6, out...  2.28 us

profile of v2, /device:TPU:1, one launch (start us, length us, event | category | flops | bytes accessed | tf_op | source)
XLA Modules:
  0.0 62.9 jit_solution(13617581759772166355)
XLA Ops:
  0.6 59.8 %shard_map.127 = (bf16[1,128,1024]{2,1,0:T(8,128)(2,1)}, bf16[1,128,1024]{2,1,0:T(8,128)(2,1)}, bf16[1,128,1024]{2,1,0:T(8,128)(2,1)}, bf16[1,128,1024]{2,1,0:T(...) custom-call(s32[1,4]{1,0:T(1,128)} %lens.1, bf16[1,128,1024]{2,1,0:T(8,128)(2,1)} %q_in.1, ...), custom_call_target="tpu_custom_call" | custom-call | tf_op jit(solution)/shard_map/pallas_call | solution.py:471
  60.5 2.3 %shard_map.128 = (bf16[1,128,1024]{2,1,0:T(8,128)(2,1)}, bf16[1,128,1024]{2,1,0:T(8,128)(2,1)}, bf16[1,128,1024]{2,1,0:T(8,128)(2,1)}, bf16[1,128,1024]{2,1,0:T(...) custom-call(bf16[1,128,1024]{2,1,0:T(8,128)(2,1)} %get-tuple-element.18.refs_0_, ...), custom_call_target="tpu_custom_call" | custom-call | tf_op jit(solution)/shard_map/pallas_call | solution.py:513

commit v3 on v2

--- a/solution.py
+++ b/solution.py
@@ -14,11 +14,12 @@
 TOKENS = N * B
 WIDTH = 4096
 PART = WIDTH // 4
+HALF = PART // 2
 SCALE = N**-0.5
 Q, K, U, V, DO = range(5)
 FIELDS = {
     "uu": ((N, N), f32), "uk": ((N, N), f32), "inner": ((N, N), f32), "r_row": ((1, N), f32), "r_col": ((N, 1), f32),
-    "b_col": ((N, 1), f32), "across": ((N, N), bf16), "inv": ((N, N), bf16), "yc": ((N, 2 * N), bf16),
+    "b_col": ((N, 1), f32), "across": ((N, N), bf16), "inv": ((N, N), bf16), "inv_low": ((N, N), bf16), "yc": ((N, 2 * N), bf16),
     "qhat": ((N, N), bf16), "move": ((N, N), bf16), "ktil": ((N, N), bf16), "d_inner": ((N, N), bf16),
     "d_qbar": ((N, N), f32), "d_ktil": ((N, N), f32), "d_move": ((N, N), bf16),
 }
@@ -68,21 +69,22 @@
     return row, col, row == col, row > col, col <= row
 
 
-def block_forward(c, ins, logit, f):
-    query, keys, raw = (ins[a, pl.ds(c * N, N)] for a in (Q, K, U))
-    row, col, eye, before, within = masks()
-    prods = nt(down(raw, query), down(raw, keys))
-    yield
-    uu, uk, qu, qk = prods[:N, :N], prods[:N, N:], prods[N:, :N], prods[N:, N:]
+def nn3_split(a, b):
+    (ah, al), (bh, bl) = a, split(b)
+    return nn(beside(ah, al), down(bh, bh)) + nn(ah, bl)
+
+
+def block_inverse(c, ins, logit, f):
+    raw = ins[U, pl.ds(c * N, N)]
+    row, col, eye, before, _ = masks()
+    uu = nt(raw, raw)
+    yield
     diag = jnp.where(eye, uu, 0.0)
     r_row = lax.rsqrt(jnp.sum(diag, 0, keepdims=True) + 1e-6)
     r_col = lax.rsqrt(jnp.sum(diag, 1, keepdims=True) + 1e-6)
     b_row = 2.0 / (1.0 + jnp.exp(-logit))
     b_col = jnp.sum(jnp.where(eye, b_row, 0.0), 1, keepdims=True)
-    br = b_col * r_col
-    lower = jnp.where(before, br * uu * r_row, 0.0)
-    right = jnp.where(before, br * uk, 0.0)
-    across = jnp.where(within, qu * r_row, 0.0)
+    lower = jnp.where(before, b_col * r_col * uu * r_row, 0.0)
     inv = jnp.where(eye, 1.0, jnp.where((row >> 1) == (col >> 1), -lower, 0.0))
     for level in range(1, 7):
         mask = ((row >> (level + 1)) == (col >> (level + 1))) & ((row >> level) != (col >> level))
@@ -90,7 +92,21 @@
         yield
         inv = inv - nn3(half, inv)
         yield
-    yc = nn3(inv, beside(br * raw.astype(f32), right))
+    f["uu"][c], f["r_row"][c], f["r_col"][c], f["b_col"][c] = uu, r_row, r_col, b_col
+    f["inv"][c], f["inv_low"][c] = split(inv)
+
+
+def block_forward(c, ins, f):
+    query, keys, raw = (ins[a, pl.ds(c * N, N)] for a in (Q, K, U))
+    _, _, eye, before, within = masks()
+    prods = nt(down(raw, query), down(raw, keys))
+    yield
+    uk, qu, qk = prods[:N, N:], prods[N:, :N], prods[N:, N:]
+    r_col = f["r_col"][c]
+    br = f["b_col"][c] * r_col
+    right = jnp.where(before, br * uk, 0.0)
+    across = jnp.where(within, qu * f["r_row"][c], 0.0)
+    yc = nn3_split((f["inv"][c], f["inv_low"][c]), beside(br * raw.astype(f32), right))
     yield
     eyc = nn3(across, yc)
     yield
@@ -98,10 +114,10 @@
     inner = qk - eyc[:, N:]
     high, low = split(yc * r_col)
     shift = tn(down(high, low), down(raw, raw))
+    yield
     move = jnp.where(eye, 1.0, 0.0) - shift[:N]
     key_tilde = keys.astype(f32) - shift[N:]
-    f["uu"][c], f["uk"][c], f["r_row"][c], f["r_col"][c], f["b_col"][c] = uu, uk, r_row, r_col, b_col
-    f["across"][c], f["inv"][c], f["yc"][c] = across.astype(bf16), inv.astype(bf16), yc.astype(bf16)
+    f["uk"][c], f["across"][c], f["yc"][c] = uk, across.astype(bf16), yc.astype(bf16)
     f["qhat"][c], f["move"][c], f["ktil"][c] = query_bar.astype(bf16), move.astype(bf16), key_tilde.astype(bf16)
     f["inner"][c] = inner
 
@@ -159,7 +175,7 @@
 def kernel(
     lens, q_in, k_in, v_in, u_in, l_in, proj, grad,
     dq_out, dk_out, dv_out, du_out, gp_out, dl_out,
-    ins, logits, grad_own, proj_own, dout_own, grad_z, grad_y, att_own, att, att_z, att_y, made, dl_made, dl_got, prod, rs_first, mid, rs_last, fin,
+    ins, logits, grad_own, proj_own, dout_own, grad_z, grad_y, att_own, att, att_z, att_y, made, dl_made, dl_got, prod, rs_first, mid, rs_last,
     in_send, in_recv, out_send, out_recv, att_send, att_recv, rs_send, rs_recv, fin_send, fin_recv, here, *parts,
 ):
     f = dict(zip(FIELDS, parts))
@@ -201,15 +217,20 @@
     own = [local(ref.at[0, :, cols(me)], ins.at[a, rows], here.at[a]) for a, ref in sources.items()]
     own.append(local(l_in.at[0], logits.at[me], here.at[4]))
     own_grad = local(grad.at[0], grad_own, here.at[5])
+    z_half, y_half = lax.rem(pz, 2), lax.rem(py, 2)
+    z_for, y_for = pz - z_half + core, py - y_half + core
     z_rows, y_rows = (pl.ds(pl.multiple_of(slot * N, N), N) for slot in (z_slot, y_slot))
     own_cut = [
-        local(grad.at[0, :, cols(core, PART)], grad_z.at[z_rows], here.at[6]),
-        local(grad.at[0, :, cols(core + 2, PART)], grad_y.at[y_rows], here.at[22]),
+        local(grad.at[0, :, cols(z_half, PART)], grad_z.at[z_rows], here.at[6]),
+        local(grad.at[0, :, cols(y_half + 2, PART)], grad_y.at[y_rows], here.at[22]),
     ]
     own_proj = [local(proj.at[cols(x_at[dx], 2 * N)], proj_own.at[dx], here.at[8 + dx]) for dx in range(4)]
 
     barrier = pltpu.get_barrier_semaphore()
     greeted = [(dp, p) for p in peers[1:]] + [d for _, d, _ in y_group[2:] + z_group[2:]]
+    z_pair, y_pair = pz + 1 - 2 * z_half, py + 1 - 2 * y_half
+    for chip in (py * 4 + z_pair, y_pair * 4 + pz):
+        greeted += [(chip, p) for p in peers[2:]]
     for device in greeted:
         pl.semaphore_signal(barrier, inc=1, device_id=device, device_id_type=MESH)
     pl.semaphore_wait(barrier, len(greeted))
@@ -223,31 +244,29 @@
             src, dst = sources[a].at[0, :, cols(peers[o])], ins.at[a, rows]
         got[a, o] = send(src, dst, in_send.at[a, o], in_recv.at[a, o], (dp, peers[o]))
 
-    for near in (NEAR, NEXT, FAR):
-        for a in (U, K, Q, 5):
-            for o in near:
-                send_in(a, o)
-    for o in (*NEXT, *FAR, *NEAR):
-        send_in(V, o)
-
-    for o in range(1, B):
-        c, to, _ = z_group[o]
-        got[6, o] = send(grad.at[0, :, cols(c, PART)], grad_z.at[z_rows], in_send.at[6, o], in_recv.at[6, o], to)
-        c, to, _ = y_group[o]
-        got[7, o] = send(grad.at[0, :, cols(c + 2, PART)], grad_y.at[y_rows], in_send.at[7, o], in_recv.at[7, o], to)
+    for a in (5, U, K, Q):
+        for o in (*NEXT, *FAR, *NEAR):
+            send_in(a, o)
+
+    for o in range(1, 4):
+        half = lax.rem(z_at[o], 2)
+        got[6, o] = send(
+            grad.at[0, :, cols(half, PART)], grad_z.at[z_rows], in_send.at[6, o], in_recv.at[6, o], along_z[o]
+        )
+        half = lax.rem(y_at[o], 2)
+        got[7, o] = send(
+            grad.at[0, :, cols(half + 2, PART)], grad_y.at[y_rows], in_send.at[7, o], in_recv.at[7, o], along_y[o]
+        )
+    got[6, 4] = send(
+        grad.at[0, :, cols(z_half, PART)], grad_z.at[z_rows], in_send.at[6, 4], in_recv.at[6, 4], (dp, sibling)
+    )
+    got[7, 4] = send(
+        grad.at[0, :, cols(y_half + 2, PART)], grad_y.at[y_rows], in_send.at[7, 4], in_recv.at[7, 4], (dp, sibling)
+    )
 
     for copy in own:
         copy.wait()
     head = lax.broadcasted_iota(jnp.int32, (B, N), 0) == me
-
-    def forward_of(blocks, arrivals):
-        for a in (U, K, Q, 5):
-            for o in arrivals:
-                got[a, o].wait_recv()
-        own_logits = [jnp.sum(jnp.where(head, logits[c], 0.0), 0, keepdims=True) for c in blocks]
-        together(block_forward(c, ins, logit, f) for c, logit in zip(blocks, own_logits))
-
-    forward_of([peers[o] for o in (0, 1)], NEAR)
 
     own_grad.wait()
     for dx in (1, 3, 2, 0):
@@ -255,19 +274,26 @@
         both = nt(grad_own[...], proj_own[dx]).astype(bf16)
         for c in range(2):
             dout_own[dx, c] = both[:, c * N : (c + 1) * N]
-        for o in (2 * dx, 2 * dx + 1):
-            if o:
-                src = dout_own.at[dx, lax.rem(peers[o], 2)]
-                got[DO, o] = send(src, ins.at[DO, rows], in_send.at[DO, o], in_recv.at[DO, o], (dp, peers[o]))
     own_dout = local(dout_own.at[0, core], ins.at[DO, rows], here.at[7])
 
-    forward_of([peers[o] for o in NEXT + FAR], NEXT + FAR)
+    for a in (5, U):
+        for o in range(1, B):
+            got[a, o].wait_recv()
+    own_logits = [jnp.sum(jnp.where(head, logits[c], 0.0), 0, keepdims=True) for c in range(B)]
+    for o in (*NEXT, *FAR, *NEAR):
+        send_in(V, o)
+    for o in (*NEXT, *FAR, *NEAR):
+        src = dout_own.at[o // 2, lax.rem(peers[o], 2)]
+        got[DO, o] = send(src, ins.at[DO, rows], in_send.at[DO, o], in_recv.at[DO, o], (dp, peers[o]))
+    together(block_inverse(c, ins, own_logits[c], f) for c in range(B))
+    for a in (K, Q):
+        for o in range(1, B):
+            got[a, o].wait_recv()
+    together(block_forward(c, ins, f) for c in range(B))
 
     def block(a, c):
         return ins[a, c * N : (c + 1) * N]
 
-    for o in range(1, B):
-        got[V, o].wait_recv()
     ends = [lens[0, 0]]
     for i in range(1, 4):
         ends.append(ends[-1] + lens[0, i])
@@ -298,11 +324,17 @@
         mass = jnp.sum(part, 1, keepdims=True)
         yield
         probs[c] = part * (1.0 / mass)
-        result = nn(probs[c], ins[V, :span])
+        yield
+
+    def row_result(c):
+        result = nn(probs[c], ins[V, : (c + 1) * N])
         yield
         att_own[c] = result.T.astype(bf16).reshape(2, 64, N)
 
     together([carry_on(), *(row_forward(c) for c in range(B))])
+    for o in range(1, B):
+        got[V, o].wait_recv()
+    together(row_result(c) for c in range(B))
 
     own_att = local(att_own.at[me], att.at[lax.div(me, 2), pl.ds(lax.rem(me, 2) * 2, 2)], here.at[23])
     att_got = []
@@ -313,6 +345,12 @@
                 att_send.at[0, o], att_recv.at[0, o], (dp, peers[o]),
             )
         )
+
+    for o in range(1, 4):
+        for a, at, place in ((6, z_at, grad_z), (7, y_at, grad_y)):
+            got[a, o].wait_recv()
+            part = place.at[pl.ds(pl.multiple_of((at[4 - o] * 2 + core) * N, N), N)]
+            got[a, 4 + o] = send(part, part, in_send.at[a, 4 + o], in_recv.at[a, 4 + o], (dp, sibling))
 
     own_dout.wait()
     for o in range(1, B):
@@ -381,14 +419,16 @@
     for copy in att_got:
         copy.wait_recv()
     own_share = [
-        local(att.at[:, pz], att_z.at[z_slot], here.at[24]),
-        local(att.at[py], att_y.at[y_slot], here.at[25]),
+        local(att.at[:, z_for], att_z.at[z_slot], here.at[24]),
+        local(att.at[y_for], att_y.at[y_slot], here.at[25]),
     ]
     shared = []
     for o in range(1, B):
-        _, to, z = z_group[o]
+        c, to, z = z_group[o]
+        z = z - lax.rem(z, 2) + c
         shared.append(send(att.at[:, z], att_z.at[z_slot], att_send.at[1, o], att_recv.at[1, o], to))
-        _, to, y = y_group[o]
+        c, to, y = y_group[o]
+        y = y - lax.rem(y, 2) + c
         shared.append(send(att.at[y], att_y.at[y_slot], att_send.at[2, o], att_recv.at[2, o], to))
 
     for some in (NEXT, FAR + (1, 0)):
@@ -406,49 +446,87 @@
 
     for copy in own_cut + own_share:
         copy.wait()
-    for o in range(1, B):
+    for o in range(4, B):
         got[6, o].wait_recv()
         got[7, o].wait_recv()
     for copy in shared:
         copy.wait_recv()
-    for i, (left, right) in enumerate(((att_z, grad_z), (att_y, grad_y))):
-        rows_of = beside(*(left[m].reshape(2 * N, N) for m in range(B)))
-        prod[i] = nn(rows_of, right[...]).astype(bf16).reshape(4, 64, PART)
-
-    first = []
-    for o in range(1, 4):
-        first.append(send(prod.at[0, y_at[o]], rs_first.at[0, o - 1], rs_send.at[0, o], rs_recv.at[0, o], along_y[o]))
-        first.append(send(prod.at[1, z_at[o]], rs_first.at[1, o - 1], rs_send.at[1, o], rs_recv.at[1, o], along_z[o]))
-    for copy in first:
-        copy.wait_recv()
-    for i, own in enumerate((py, pz)):
-        part = prod[i, own].astype(f32) + sum(rs_first[i, o].astype(f32) for o in range(3))
-        mid[:, i] = part.astype(bf16).reshape(4, 16, PART)
-    last = []
-    for o in range(1, 4):
-        last.append(send(mid.at[x_at[o]], rs_last.at[o - 1], rs_send.at[2, o], rs_recv.at[2, o], along_x[o]))
-    for copy in last:
-        copy.wait_recv()
-    total = mid[px].astype(f32) + sum(rs_last[o].astype(f32) for o in range(3))
-    for c in range(2):
-        fin[c] = total[:, c * 8 : c * 8 + 8]
-    gp_own, gp_got = [], []
-    for i in range(2):
-        place = cols(core + 2 * i, PART)
-        gp_own.append(local(fin.at[core, i], gp_out.at[:, place], here.at[26 + i]))
-        gp_got.append(
-            send(fin.at[1 - core, i], gp_out.at[:, place], fin_send.at[i], fin_recv.at[i], (dp, sibling))
+    att_rows = [beside(*(a[m].reshape(2 * N, N) for m in range(B))) for a in (att_z, att_y)]
+    first = {}
+    for h in range(2):
+        for i, place in enumerate((grad_z, grad_y)):
+            prod[i, h] = nn(att_rows[i], place[:, h * HALF : (h + 1) * HALF]).astype(bf16).reshape(4, 64, HALF)
+            for o in range(1, 4):
+                at, to = (y_at[o], along_y[o]) if i == 0 else (z_at[o], along_z[o])
+                first[h, i, o] = send(
+                    prod.at[i, h, at], rs_first.at[i, h, o - 1], rs_send.at[2 * i + h, o], rs_recv.at[2 * i + h, o], to
+                )
+    halves, owners = (z_half, y_half), (py * 4 + z_for, y_for * 4 + pz)
+
+    def last_copy(h, i, dx, c):
+        return pltpu.make_async_remote_copy(
+            src_ref=mid.at[h, i, x_at[dx], c], dst_ref=rs_last.at[h, i, halves[i], dx],
+            send_sem=fin_send.at[4 * h + 2 * i + c, dx], recv_sem=fin_recv.at[4 * h + 2 * i + halves[i], dx],
+            device_id=(owners[i], x_at[dx] * 2 + c), device_id_type=MESH,
         )
+
+    def self_copy(h, i, c):
+        return pltpu.make_async_copy(mid.at[h, i, px, c], rs_last.at[h, i, halves[i], 0], here.at[26 + 2 * h + i])
+
+    def unless_own(i, c, own_step, step):
+        own_one = jnp.logical_and(core == halves[i], core == c)
+        pl.when(own_one)(own_step)
+        pl.when(jnp.logical_not(own_one))(step)
+
+    for h in range(2):
+        for i, own in enumerate((py, pz)):
+            for o in range(1, 4):
+                first[h, i, o].wait_recv()
+            part = prod[i, h, own].astype(f32) + sum(rs_first[i, h, o].astype(f32) for o in range(3))
+            for x in range(4):
+                for c in range(2):
+                    at = (2 * x + c) * 8
+                    tile = part[at : at + 8]
+                    mid[h, i, x, c] = down(tile[:, : HALF // 2], tile[:, HALF // 2 :]).astype(bf16)
+            for dx in (1, 3, 2):
+                for c in range(2):
+                    last_copy(h, i, dx, c).start()
+            for c in range(2):
+                unless_own(
+                    i, c, functools.partial(lambda *a: self_copy(*a).start(), h, i, c),
+                    functools.partial(lambda *a: last_copy(*a).start(), h, i, 0, c),
+                )
+    for h in range(2):
+        for i in range(2):
+            for source in range(2):
+                for dx in range(4):
+                    arrival = pltpu.make_async_remote_copy(
+                        src_ref=mid.at[h, i, 0, 0], dst_ref=rs_last.at[h, i, source, dx],
+                        send_sem=fin_send.at[4 * h + 2 * i, dx], recv_sem=fin_recv.at[4 * h + 2 * i + source, dx],
+                        device_id=(dp, sibling), device_id_type=MESH,
+                    )
+                    if dx:
+                        arrival.wait_recv()
+                    else:
+                        own_one = jnp.logical_and(core == halves[i], core == source)
+                        pl.when(own_one)(functools.partial(lambda *a: self_copy(*a).wait(), h, i, source))
+                        pl.when(jnp.logical_not(own_one))(arrival.wait_recv)
+                total = sum(rs_last[h, i, source, dx].astype(f32) for dx in range(4))
+                at = (2 * i + source) * PART + h * HALF
+                gp_out[:, at : at + HALF // 2] = total[:8]
+                gp_out[:, at + HALF // 2 : at + HALF] = total[8:]
 
     for i in range(5):
         out[i, 0].wait()
         for o in range(1, B):
             out[i, o].wait_recv()
     dl_out[0] = sum(dl_got[h] for h in range(B))
-    for copy in gp_own:
-        copy.wait()
-    for copy in gp_got:
-        copy.wait_recv()
+    for h in range(2):
+        for i in range(2):
+            for c in range(2):
+                for dx in range(1, 4):
+                    last_copy(h, i, dx, c).wait_send()
+                unless_own(i, c, lambda: None, functools.partial(lambda *a: last_copy(*a).wait_send(), h, i, 0, c))
     for copy in sent:
         copy.wait_send()
 
@@ -472,7 +550,7 @@
         kernel,
         out_shape=results,
         in_specs=[pl.BlockSpec(memory_space=pltpu.SMEM)] + [anywhere] * 7,
-        out_specs=[anywhere] * 5 + [pl.BlockSpec(memory_space=pltpu.VMEM)],
+        out_specs=[anywhere] * 4 + [pl.BlockSpec(memory_space=pltpu.VMEM)] * 2,
         scratch_shapes=[
             pltpu.VMEM((5, TOKENS, N), bf16),
             pltpu.VMEM((B, B, N), f32),
@@ -488,11 +566,10 @@
             pltpu.VMEM((4, TOKENS, N), bf16),
             pltpu.VMEM((B, B, N), f32),
             pltpu.VMEM((B, B, N), f32),
-            pltpu.VMEM((2, 4, 64, PART), bf16),
-            pltpu.VMEM((2, 3, 64, PART), bf16),
-            pltpu.VMEM((4, 2, 16, PART), bf16),
-            pltpu.VMEM((3, 2, 16, PART), bf16),
-            pltpu.VMEM((2, 2, 8, PART), f32),
+            pltpu.VMEM((2, 2, 4, 64, HALF), bf16),
+            pltpu.VMEM((2, 2, 3, 64, HALF), bf16),
+            pltpu.VMEM((2, 2, 4, 2, 16, HALF // 2), bf16),
+            pltpu.VMEM((2, 2, 2, 4, 16, HALF // 2), bf16),
             dma((8, B)),
             dma((8, B)),
             dma((5, B)),
@@ -501,9 +578,9 @@
             dma((3, B)),
             dma((4, 4)),
             dma((4, 4)),
-            dma((2,)),
-            dma((2,)),
-            dma((28,)),
+            dma((B, 4)),
+            dma((B, 4)),
+            dma((30,)),
             *(pltpu.VMEM((B, *shape), dtype) for shape, dtype in FIELDS.values()),
         ],
         compiler_params=pltpu.CompilerParams(

time: 63 us -> 59.3 us (0.941)
  Pallas kernels: 62.1 us -> 58.3 us
    pallas_call x1, Pallas kernels: 59.8 us -> 56 us  [per_device(): pl.pallas_call(kernel, out_shape=results, in_specs=[pl.BlockSpec(memory_s...]
where the time goes in v3:
time: 59.3 us; the launch traced here: 59.1 us
  Pallas kernels  58.3 us (98%)
  between operations  0.8 us (1%)
    pallas_call x1, Pallas kernels, per_device(): pl.pallas_call(kernel, out_shape=results, in_specs=[pl.BlockSpec(memory_s...  56 us
    pallas_call x1, Pallas kernels, per_device(): pl.pallas_call(hand_over, out_shape=results, in_specs=[anywhere] * 6, out...  2.28 us

profile of v3, /device:TPU:1, one launch (start us, length us, event | category | flops | bytes accessed | tf_op | source)
XLA Modules:
  0.0 59.1 jit_solution(14512082587077164955)
XLA Ops:
  0.6 56.0 %shard_map.127 = (bf16[1,128,1024]{2,1,0:T(8,128)(2,1)}, bf16[1,128,1024]{2,1,0:T(8,128)(2,1)}, bf16[1,128,1024]{2,1,0:T(8,128)(2,1)}, bf16[1,128,1024]{2,1,0:T(...) custom-call(s32[1,4]{1,0:T(1,128)} %lens.1, bf16[1,128,1024]{2,1,0:T(8,128)(2,1)} %q_in.1, ...), custom_call_target="tpu_custom_call" | custom-call | tf_op jit(solution)/shard_map/pallas_call | solution.py:549
  56.7 2.3 %shard_map.128 = (bf16[1,128,1024]{2,1,0:T(8,128)(2,1)}, bf16[1,128,1024]{2,1,0:T(8,128)(2,1)}, bf16[1,128,1024]{2,1,0:T(8,128)(2,1)}, bf16[1,128,1024]{2,1,0:T(...) custom-call(bf16[1,128,1024]{2,1,0:T(8,128)(2,1)} %get-tuple-element.18.refs_0_, ...), custom_call_target="tpu_custom_call" | custom-call | tf_op jit(solution)/shard_map/pallas_call | solution.py:590

commit v4 on v3

--- a/solution.py
+++ b/solution.py
@@ -135,7 +135,8 @@
     yield
     d_across = jnp.where(within, -nt(d_qi, yc), 0.0).astype(bf16)
     yield
-    d_br = tn(f["inv"][c], d_yc)
+    high, low = split(d_yc)
+    d_br = tn(down(f["inv"][c], f["inv_low"][c]), down(high, high)) + tn(f["inv"][c], low)
     yield
     d_lower = jnp.where(before, -nt(d_br, yc), 0.0)
     yield
@@ -352,6 +353,22 @@
             part = place.at[pl.ds(pl.multiple_of((at[4 - o] * 2 + core) * N, N), N)]
             got[a, 4 + o] = send(part, part, in_send.at[a, 4 + o], in_recv.at[a, 4 + o], (dp, sibling))
 
+    own_att.wait()
+    for copy in att_got:
+        copy.wait_recv()
+    own_share = [
+        local(att.at[:, z_for], att_z.at[z_slot], here.at[24]),
+        local(att.at[y_for], att_y.at[y_slot], here.at[25]),
+    ]
+    shared = []
+    for o in range(1, B):
+        c, to, z = z_group[o]
+        z = z - lax.rem(z, 2) + c
+        shared.append(send(att.at[:, z], att_z.at[z_slot], att_send.at[1, o], att_recv.at[1, o], to))
+        c, to, y = y_group[o]
+        y = y - lax.rem(y, 2) + c
+        shared.append(send(att.at[y], att_y.at[y_slot], att_send.at[2, o], att_recv.at[2, o], to))
+
     own_dout.wait()
     for o in range(1, B):
         got[DO, o].wait_recv()
@@ -414,22 +431,6 @@
         made[3, j * N : (j + 1) * N] = d_value[j].astype(bf16)
     for o in (*NEXT, *FAR, *NEAR, 0):
         send_out(3, o)
-
-    own_att.wait()
-    for copy in att_got:
-        copy.wait_recv()
-    own_share = [
-        local(att.at[:, z_for], att_z.at[z_slot], here.at[24]),
-        local(att.at[y_for], att_y.at[y_slot], here.at[25]),
-    ]
-    shared = []
-    for o in range(1, B):
-        c, to, z = z_group[o]
-        z = z - lax.rem(z, 2) + c
-        shared.append(send(att.at[:, z], att_z.at[z_slot], att_send.at[1, o], att_recv.at[1, o], to))
-        c, to, y = y_group[o]
-        y = y - lax.rem(y, 2) + c
-        shared.append(send(att.at[y], att_y.at[y_slot], att_send.at[2, o], att_recv.at[2, o], to))
 
     for some in (NEXT, FAR + (1, 0)):
         blocks = [peers[o] for o in some]

time: 59.3 us -> 59.3 us (level)
  no operation moved by 1% of the time
where the time goes in v4:
time: 59.3 us; the launch traced here: 59.1 us
  Pallas kernels  58.3 us (98%)
  between operations  0.82 us (1%)
    pallas_call x1, Pallas kernels, per_device(): pl.pallas_call(kernel, out_shape=results, in_specs=[pl.BlockSpec(memory_s...  56 us
    pallas_call x1, Pallas kernels, per_device(): pl.pallas_call(hand_over, out_shape=results, in_specs=[anywhere] * 6, out...  2.28 us

profile of v4, /device:TPU:1, one launch (start us, length us, event | category | flops | bytes accessed | tf_op | source)
XLA Modules:
  0.0 59.1 jit_solution(5744967329951344961)
XLA Ops:
  0.6 56.0 %shard_map.127 = (bf16[1,128,1024]{2,1,0:T(8,128)(2,1)}, bf16[1,128,1024]{2,1,0:T(8,128)(2,1)}, bf16[1,128,1024]{2,1,0:T(8,128)(2,1)}, bf16[1,128,1024]{2,1,0:T(...) custom-call(s32[1,4]{1,0:T(1,128)} %lens.1, bf16[1,128,1024]{2,1,0:T(8,128)(2,1)} %q_in.1, ...), custom_call_target="tpu_custom_call" | custom-call | tf_op jit(solution)/shard_map/pallas_call | solution.py:550
  56.7 2.3 %shard_map.128 = (bf16[1,128,1024]{2,1,0:T(8,128)(2,1)}, bf16[1,128,1024]{2,1,0:T(8,128)(2,1)}, bf16[1,128,1024]{2,1,0:T(8,128)(2,1)}, bf16[1,128,1024]{2,1,0:T(...) custom-call(bf16[1,128,1024]{2,1,0:T(8,128)(2,1)} %get-tuple-element.18.refs_0_, ...), custom_call_target="tpu_custom_call" | custom-call | tf_op jit(solution)/shard_map/pallas_call | solution.py:591
